TPU v7x, 256 devices: a whole 4x4x8 slice. The times are simulated.
256 devices in a mesh: fsdp: 8 (over y, core), tp: 8 (over z), rep: 4 (over x).
Axes of the slice: x: 4, y: 4, z: 8, core: 2. Of those that a mesh axis runs over, the one named last changes fastest.
Arguments:
- train_inputs: bfloat16 [20480, 8192], P(('fsdp', 'rep'), 'tp'), may hold values from -6 to 6
- kv_grads: bfloat16 [20480, 2048], P(('fsdp', 'rep'), 'tp'), may hold values from -0.125 to 0.125
- master: float32 [8192, 2048], P(('fsdp', 'rep'), 'tp'), may hold values from -0.0234375 to 0.0234375
- first_moment: bfloat16 [8192, 2048], P(('fsdp', 'rep'), 'tp'), may hold values from -0.29882812 to 0.29882812
- second_moment: bfloat16 [8192, 2048], P(('fsdp', 'rep'), 'tp'), may hold values from 0.019897461 to 0.31835938
- hidden_states: bfloat16 [4, 1024, 8192], P(None, ('fsdp', 'rep')), may hold values from -18 to 18
- queries: bfloat16 [4, 1024, 8192], P(None, ('fsdp', 'rep'), 'tp'), may hold values from -24 to 24
- kv_cache: bfloat16 [1024, 256, 2048], P(('fsdp', 'rep'), None, 'tp'), may hold values from -24 to 24
- cache_lengths: int32 [1024], P(('fsdp', 'rep')), may hold values from 2 to 256, as said below
Outputs:
- new_master: float32 [8192, 2048], P(('fsdp', 'rep'), 'tp')
- new_first: bfloat16 [8192, 2048], P(('fsdp', 'rep'), 'tp')
- new_second: bfloat16 [8192, 2048], P(('fsdp', 'rep'), 'tp')
- attended: bfloat16 [4, 1024, 8192], P(None, ('fsdp', 'rep'), 'tp')
Inputs may be any that keep to these rules, and one draw needn't show every extreme that they name: `cache_lengths`: in the first row of every device's 32 rows all 256 slots are live.
All inputs are finite; a program needn't handle non-finite values.
Results may differ from a plain program's by a relative error of at most 0.0055.
Values may be sent and summed in bfloat16 or wider, within the bound.
No kernel may reach another device: no remote copies, remote signals or barrier semaphores. Data moves between devices by JAX's collectives and lax.ppermute only.
A program may use at most 128 MiB of HBM per device.

v0:
```python
import functools
import math

import jax
import jax.numpy as jnp
from jax import lax
from jax.experimental import pallas as pl
from jax.experimental.pallas import tpu as pltpu
from jax.sharding import PartitionSpec as P

HEADS = 64
KVH = 8
HD = 128
ADAM_STEP = 100

learn_rate = 0.001
beta_one = 0.9
beta_two = 0.95
decay_rate = 0.1
tiny_term = 1e-08

NY, NX, NZ = 4, 4, 8
AXES = ("fsdp", "tp", "rep")
VMEM_LIMIT = 40 * 1024 * 1024
f32 = jnp.float32
bf16 = jnp.bfloat16


def pairs_of(move):
    pairs = []
    for y in range(NY):
        for k in range(2):
            for x in range(NX):
                for z in range(NZ):
                    v, j, u, w = move(y, k, x, z)
                    source = ((y * 2 + k) * NZ + z) * NX + x
                    target = (((v % NY) * 2 + j) * NZ + w % NZ) * NX + u % NX
                    pairs.append((source, target))
    return pairs


def swap_core(a):
    return lax.ppermute(a, AXES, pairs_of(lambda y, k, x, z: (y, 1 - k, x, z)))


def pass_on(a):
    return lax.ppermute(a, AXES, pairs_of(lambda y, k, x, z: (y, k, x, z + 1 - 2 * k)))


def pass_last(a):
    pairs = pairs_of(lambda y, k, x, z: (y, k, x, z - 1))
    return lax.ppermute(a, AXES, [m for m in pairs if m[0] // (NX * NZ) % 2 == 1])


def shift_first(a, d):
    return lax.ppermute(
        a, AXES, pairs_of(lambda y, k, x, z: (y, k, x + d, z) if k == 0 else (y + d, k, x, z))
    )


def shift_second(a, d):
    return lax.ppermute(
        a, AXES, pairs_of(lambda y, k, x, z: (y + d, k, x, z) if k == 0 else (y, k, x + d, z))
    )


def to_owner(a):
    return lax.ppermute(
        a, AXES, pairs_of(lambda y, k, x, z: (z // 2, z % 2, x, z + 4 * k - y))
    )


SMEM = pl.BlockSpec(memory_space=pltpu.SMEM)
VMEM = pl.BlockSpec(memory_space=pltpu.VMEM)
ANY = pl.BlockSpec(memory_space=pl.ANY)


def call(kernel, out, args, in_specs, out_specs, scratch=(), aliases=None, flops=0, moved=0):
    return pl.pallas_call(
        kernel,
        out_shape=out,
        in_specs=in_specs,
        out_specs=out_specs,
        scratch_shapes=list(scratch),
        input_output_aliases=aliases or {},
        cost_estimate=pl.CostEstimate(flops=flops, bytes_accessed=moved, transcendentals=0),
        compiler_params=pltpu.CompilerParams(vmem_limit_bytes=VMEM_LIMIT),
    )(*args)


def shape(dims, dtype):
    return jax.ShapeDtypeStruct(dims, dtype)


def after_all(value, *others):
    def kernel(*refs):
        pass

    return call(
        kernel,
        shape(value.shape, value.dtype),
        (value, *others),
        [ANY] * (1 + len(others)),
        ANY,
        aliases={0: 0},
    )


def partial_kernel(step, *refs):
    place, own_x, other_x, block, other_block = refs[:5]
    keep, one, two, three, token, turned = refs[-6:]
    k, p = place[0], place[1]
    slot = jnp.where(k == 0, step, 4 - step)
    token[...] = jnp.zeros_like(token)

    @pl.when((slot >= 0) & (slot < 4))
    def _():
        turned[0] = block[...].T
        turned[1] = other_block[...].T

        def one_tile(i, carry):
            a = jnp.where(k == 0, lax.rem(p + i, 4), i)
            d = jnp.where(k == 0, i, lax.rem(slot - p + 4, 4))
            index = jnp.where(k == 0, slot, i)
            at = pl.ds(pl.multiple_of(a * 256, 256), 256)
            tile = jnp.dot(turned[0], own_x[:, at], preferred_element_type=f32)
            tile = tile + jnp.dot(turned[1], other_x[:, at], preferred_element_type=f32)

            @pl.when(d == 0)
            def _():
                keep[index] = tile

            for m, out in ((1, one), (2, two), (3, three)):

                @pl.when(d == m)
                def _():
                    out[index] = tile.astype(bf16)

            return carry

        lax.fori_loop(0, 4, one_tile, 0)


def middle_kernel(place, keep, one, two, three, *refs):
    own, s_one, s_two, s_three = refs[3:]
    q = place[2]
    for d, out in enumerate((own, s_one, s_two, s_three)):
        j = lax.rem(q + d, 4)
        out[...] = (
            keep[j] + one[j].astype(f32) + two[j].astype(f32) + three[j].astype(f32)
        ).astype(out.dtype)


def adam_kernel(gradient, master, first_moment, second_moment, *outs):
    new_master, new_first, new_second, weight = outs
    gradient = gradient[...].astype(f32).T
    first = beta_one * first_moment[...].astype(f32) + (1.0 - beta_one) * gradient
    second = beta_two * second_moment[...].astype(f32) + (1.0 - beta_two) * gradient * gradient
    corr_one = 1.0 - beta_one**ADAM_STEP
    corr_two = 1.0 - beta_two**ADAM_STEP
    update = first / corr_one / (jnp.sqrt(second / corr_two) + tiny_term)
    update = update + decay_rate * master[...]
    result = master[...] - learn_rate * update
    new_master[...] = result
    new_first[...] = first.astype(bf16)
    new_second[...] = second.astype(bf16)
    weight[...] = result.astype(bf16)


def states_kernel(place, states, *refs):
    sends, token, sems = refs[:4], refs[4], refs[5]
    k, p, q = place[0], place[1], place[2]
    copies = []
    for m in range(4):
        for n in range(4):
            u, v = lax.rem(p + m, 4), lax.rem(q + n, 4)
            x = jnp.where(k == 0, u, v)
            y = jnp.where(k == 0, v, u)
            for i, core in enumerate((k, 1 - k)):
                at = pl.multiple_of(((2 * y + core) * 4 + x) * 256, 256)
                copies.append(
                    pltpu.make_async_copy(
                        states.at[:, pl.ds(at, 256)], sends[m].at[n, i], sems.at[len(copies)]
                    )
                )
                copies[-1].start()
    token[...] = jnp.zeros_like(token)
    for copy in copies:
        copy.wait()


def regroup_kernel(*refs):
    came, sends, token = refs[:4], refs[4:8], refs[8]
    token[...] = jnp.zeros_like(token)
    for n in range(4):
        for m in range(4):
            sends[n][m] = came[m][n]


def project_kernel(weight, other_weight, *refs):
    states, sends = refs[:4], refs[4:]
    for m, out in enumerate(sends):
        for n in range(4):
            term = jnp.dot(states[n][m, 0], weight[...], preferred_element_type=f32)
            term = term + jnp.dot(states[n][m, 1], other_weight[...], preferred_element_type=f32)
            out[n] = term.astype(out.dtype)


def gather_kernel(keep, one, two, three, *outs):
    for n, out in enumerate(outs):
        out[...] = (
            keep[n] + one[n].astype(f32) + two[n].astype(f32) + three[n].astype(f32)
        )


def finish_kernel(own, one, two, three, queries, peak, mass, past, out):
    fresh = (own[...] + one[...] + two[...] + three[...]).astype(bf16)
    n = fresh.shape[0]
    rows = n // 4
    group = HEADS // KVH
    line = lax.broadcasted_iota(jnp.int32, (n, n), 0)
    lane = lax.broadcasted_iota(jnp.int32, (n, n), 1)
    seen = (lax.rem(line, rows) == lax.rem(lane, rows)) & (lane <= line)
    seen = jnp.concatenate([seen.astype(f32)] * group, axis=0) > 0.5
    scale = 1.0 / math.sqrt(HD)
    keys, values = fresh[:, :HD], fresh[:, HD:]
    stack = jnp.concatenate([queries[:, g * HD : g * HD + HD] for g in range(group)], axis=0)
    scores = lax.dot_general(
        stack, keys, (((1,), (1,)), ((), ())), preferred_element_type=f32
    )
    scores = jnp.where(seen, scores * scale, -1e30)
    before = jnp.concatenate([peak[:, g : g + 1] for g in range(group)], axis=0)
    mass = jnp.concatenate([mass[:, g : g + 1] for g in range(group)], axis=0)
    top = jnp.maximum(before, jnp.max(scores, axis=1, keepdims=True))
    weight = jnp.where(seen, jnp.exp(scores - top), 0.0)
    fade = jnp.exp(before - top)
    total = mass * fade + jnp.sum(weight, axis=1, keepdims=True)
    probs = (weight / total).astype(bf16)
    result = jnp.dot(probs, values, preferred_element_type=f32)
    result = (result + past[...] * (fade / total)).astype(bf16)
    for g in range(group):
        out[:, g * HD : g * HD + HD] = result[g * n : g * n + n]


def past_part(queries, cache, lengths):
    steps, rows = queries.shape[0], queries.shape[1]
    span = cache.shape[1]
    group = HEADS // KVH
    block = queries.reshape(steps, rows, group, HD)
    scores = jnp.einsum(
        "srgd,rtd->srgt", block, cache[:, :, :HD], preferred_element_type=f32
    ) * (1.0 / math.sqrt(HD))
    live = jnp.arange(span, dtype=jnp.int32)[None, :] < lengths[:, None]
    scores = jnp.where(live[None, :, None, :], scores, -jnp.inf)
    peak = jnp.max(scores, axis=-1)
    weight = jnp.exp(scores - peak[..., None])
    mass = jnp.sum(weight, axis=-1)
    past = jnp.einsum(
        "srgt,rtd->gsrd", weight.astype(bf16), cache[:, :, HD:], preferred_element_type=f32
    )
    n = steps * rows
    return peak.reshape(n, group), mass.reshape(n, group), past.reshape(n * group, HD)


def body(
    train_inputs,
    kv_grads,
    master,
    first_moment,
    second_moment,
    hidden_states,
    queries,
    kv_cache,
    cache_lengths,
):
    f = lax.axis_index("fsdp")
    x = lax.axis_index("rep")
    y, k = f // 2, f % 2
    p = jnp.where(k == 0, x, y)
    q = jnp.where(k == 0, y, x)
    place = jnp.stack([k, p, q]).astype(jnp.int32)
    steps, rows, width = hidden_states.shape
    count = steps * rows

    block = kv_grads
    other_block = swap_core(kv_grads)
    other_x = swap_core(train_inputs)

    part = (4, 256, 256)
    buffers = ()
    outs = (shape(part, f32),) + (shape(part, bf16),) * 3 + (shape((8, 128), f32),)

    def add_slot(step, block, other_block, buffers, awaited=()):
        first = not buffers
        *buffers, token = call(
            functools.partial(partial_kernel, step),
            outs,
            (place, train_inputs, other_x, block, other_block, *buffers, *awaited),
            [SMEM] + [VMEM] * (4 + len(buffers)) + [ANY] * len(awaited),
            [VMEM] * 5,
            [pltpu.VMEM((2, 256, 640), bf16)],
            {} if first else {5: 0, 6: 1, 7: 2, 8: 3},
            flops=4 * 640 * 1024 * 256,
            moved=6 << 20,
        )
        return tuple(buffers), token

    group = (4, 2, count, 256)
    *sends, packed = call(
        states_kernel,
        (shape(group, bf16),) * 4 + (shape((8, 128), f32),),
        (place, hidden_states.reshape(count, width)),
        [SMEM, pl.BlockSpec(memory_space=pltpu.HBM)],
        [VMEM] * 5,
        [pltpu.SemaphoreType.DMA((32,))],
        moved=4 << 20,
    )
    other_block = after_all(other_block, packed)
    came = [sends[0]] + [shift_first(sends[d], d) for d in (1, 2, 3)]
    *sends, regrouped = call(
        regroup_kernel,
        (shape(group, bf16),) * 4 + (shape((8, 128), f32),),
        tuple(came),
        [VMEM] * 4,
        [VMEM] * 5,
        moved=4 << 20,
    )
    states = [sends[0]] + [shift_second(sends[d], d) for d in (1, 2, 3)]

    tokens = []
    arrived = (block, other_block)
    for step in range(5):
        if 0 < step < 4:
            awaited = (tokens[-1], regrouped) if step == 3 else (tokens[-1],)
            arrived = (arrived[0], after_all(arrived[1], *awaited))
        if step < 4:
            send = pass_on if step < 3 else pass_last
            after = (send(arrived[0]), send(arrived[1]))
        buffers, token = add_slot(step, *arrived, buffers)
        tokens.append(token)
        arrived = after

    keep, one, two, three = buffers
    peak, mass, past = past_part(queries, kv_cache, cache_lengths)
    two = after_all(two, *states[1:])
    one, two, three = shift_first(one, 1), shift_first(two, 2), shift_first(three, 3)
    square, narrow = shape((256, 256), f32), shape((256, 256), bf16)
    own, one, two, three = call(
        middle_kernel,
        (square, narrow, narrow, narrow),
        (place, keep, one, two, three, past, peak, mass),
        [SMEM] + [VMEM] * 4 + [ANY] * 3,
        [VMEM] * 4,
        moved=4 << 20,
    )
    one, two, three = shift_second(one, 1), shift_second(two, 2), shift_second(three, 3)
    gradient = own + one.astype(f32) + two.astype(f32) + three.astype(f32)
    gradient = gradient.astype(bf16)
    gradient = to_owner(gradient)
    new_master, new_first, new_second, weight = call(
        adam_kernel,
        (square, narrow, narrow, narrow),
        (gradient, master, first_moment, second_moment),
        [VMEM] * 4,
        [VMEM] * 4,
        moved=1 << 20,
    )

    part = (4, count, 256)
    keep, one, two, three = call(
        project_kernel,
        (shape(part, f32),) + (shape(part, bf16),) * 3,
        (weight, swap_core(weight), *states),
        [VMEM] * 6,
        [VMEM] * 4,
        flops=2 * 16 * count * 512 * 256,
        moved=4 << 20,
    )
    one, two, three = shift_first(one, -1), shift_first(two, -2), shift_first(three, -3)
    result = shape((count, 256), f32)
    own, one, two, three = call(
        gather_kernel,
        (result,) * 4,
        (keep, one, two, three),
        [VMEM] * 4,
        [VMEM] * 4,
        moved=2 << 20,
    )
    one, two, three = shift_second(one, -1), shift_second(two, -2), shift_second(three, -3)
    attended = call(
        finish_kernel,
        shape((count, queries.shape[2]), bf16),
        (own, one, two, three, queries.reshape(count, queries.shape[2]), peak, mass, past),
        [VMEM] * 8,
        VMEM,
        moved=1 << 20,
    )
    return new_master, new_first, new_second, attended.reshape(queries.shape)


def solution(mesh):
    in_specs = (
        P(("fsdp", "rep"), "tp"),
        P(("fsdp", "rep"), "tp"),
        P(("fsdp", "rep"), "tp"),
        P(("fsdp", "rep"), "tp"),
        P(("fsdp", "rep"), "tp"),
        P(None, ("fsdp", "rep"), None),
        P(None, ("fsdp", "rep"), "tp"),
        P(("fsdp", "rep"), None, "tp"),
        P(("fsdp", "rep")),
    )
    out_specs = (
        P(("fsdp", "rep"), "tp"),
        P(("fsdp", "rep"), "tp"),
        P(("fsdp", "rep"), "tp"),
        P(None, ("fsdp", "rep"), "tp"),
    )
    return jax.shard_map(body, mesh=mesh, in_specs=in_specs, out_specs=out_specs, check_vma=False)
```

profile of v0, /device:TPU:32, one launch (start us, length us, event | category | flops | bytes accessed | tf_op | source)
XLA Modules:
  0.0 113.0 jit_solution(2098701229518206629)
XLA Ops:
  1.2 1.9 %collective-permute-start.1 = (bf16[640,256]{1,0:T(8,128)(2,1)}, bf16[640,256]{1,0:T(8,128)(2,1)S(1)}, u32[]{:S(2)}, u32[]{:S(2)}) collective-permute-start(bf16[640,256]{1,0:T(8,128)(2,1)} %refs_3_.1), channel_id=1, source_target_pairs={{0,4},{4,8},{8,12},{12,16},{16,20},{20,24},{24,28},{28,0},{1,5},{5... | collective-permute-start | bytes 983048 | tf_op jit(solution)/shard_map/ppermute | solution.py:47
  3.2 1.6 %copy-done.1 = bf16[4,32,8192]{2,1,0:T(8,128)(2,1)S(1)} copy-done((bf16[4,32,8192]{2,1,0:T(8,128)(2,1)S(1)}, bf16[4,32,8192]{2,1,0:T(8,128)(2,1)}, u32[]{:S(2)}) %copy-start.1) | copy-done | bytes 2097176
  4.8 1.4 %shard_map.120 = (bf16[4,2,128,256]{3,2,1,0:T(8,128)(2,1)S(1)}, bf16[4,2,128,256]{3,2,1,0:T(8,128)(2,1)S(1)}, bf16[4,2,128,256]{3,2,1,0:T(8,128)(2,1)S(1)}, bf16...) custom-call(s32[3]{0:T(128)S(1)} %pad_add_fusion.place.refs_0_, bf16[128,8192]{1,0:T(8,128)(2,1)S(1)} %bitcast.45), custom_call_target="tpu_custom_call" | custom-call | bytes 4194304 | tf_op jit(solution)/shard_map/pallas_call | solution.py:79
  6.2 2.0 %collective-permute-start.6 = (bf16[640,256]{1,0:T(8,128)(2,1)S(1)}, bf16[640,256]{1,0:T(8,128)(2,1)S(1)}, u32[]{:S(2)}, u32[]{:S(2)}) collective-permute-start(bf16[640,256]{1,0:T(8,128)(2,1)S(1)} %shard_map.121.refs_4_), channel_id=1, source_target_pairs={{0,4},{4,8},{8,12},{12,16},{16,20},{20,24},{24,28},{28,0},{1,5},{5... | collective-permute-start | bytes 983048 | tf_op jit(solution)/shard_map/ppermute | solution.py:47
  8.2 3.0 %collective-permute-start.10 = (bf16[4,2,128,256]{3,2,1,0:T(8,128)(2,1)S(1)}, bf16[4,2,128,256]{3,2,1,0:T(8,128)(2,1)S(1)}, u32[]{:S(2)}, u32[]{:S(2)}) collective-permute-start(bf16[4,2,128,256]{3,2,1,0:T(8,128)(2,1)S(1)} %get-tuple-element.67), channel_id=1, source_target_pairs={{0,2},{4,6},{8,10},{12,14},{16,18},{20,22},{24,26},{28,30},{1,3},{... | collective-permute-start | bytes 1572872 | tf_op jit(solution)/shard_map/ppermute | solution.py:56
  12.4 3.1 %collective-permute-start.2 = (bf16[640,256]{1,0:T(8,128)(2,1)S(1)}, bf16[640,256]{1,0:T(8,128)(2,1)S(1)}, u32[]{:S(2)}, u32[]{:S(2)}) collective-permute-start(bf16[640,256]{1,0:T(8,128)(2,1)S(1)} %collective-permute-done.1.refs_3_), channel_id=1, source_target_pairs={{0,4},{4,8},{8,12},{12,16},{16,20},{20,24},{24,28},{28,0},{1,5},{5... | collective-permute-start | bytes 983048 | tf_op jit(solution)/shard_map/ppermute | solution.py:47
  16.4 2.3 %shard_map.122 = (f32[4,256,256]{2,1,0:T(8,128)S(1)}, bf16[4,256,256]{2,1,0:T(8,128)(2,1)S(1)}, bf16[4,256,256]{2,1,0:T(8,128)(2,1)S(1)}, bf16[4,256,256]{2,1,0:T(8,128)(2,1)S(1)}, f32[8,128]{1,0:T(8,128)S(1)}) custom-call(s32[3]{0:T(128)S(1)} %pad_add_fusion.place.refs_0_, bf16[640,1024]{1,0:T(8,128)(2,1)S(1)} %copy-done, ...), custom_call_target="tpu_custom_call" | custom-call | flops 671088640 | bytes 6291456 | tf_op jit(solution)/shard_map/pallas_call | solution.py:79
  20.1 2.5 %collective-permute-start.3 = (bf16[640,256]{1,0:T(8,128)(2,1)S(1)}, bf16[640,256]{1,0:T(8,128)(2,1)S(1)}, u32[]{:S(2)}, u32[]{:S(2)}) collective-permute-start(bf16[640,256]{1,0:T(8,128)(2,1)S(1)} %collective-permute-done.2.refs_3_), channel_id=1, source_target_pairs={{0,4},{4,8},{8,12},{12,16},{16,20},{20,24},{24,28},{28,0},{1,5},{5... | collective-permute-start | bytes 983048 | tf_op jit(solution)/shard_map/ppermute | solution.py:47
  22.6 2.3 %shard_map.124 = (f32[4,256,256]{2,1,0:T(8,128)S(1)}, bf16[4,256,256]{2,1,0:T(8,128)(2,1)S(1)}, bf16[4,256,256]{2,1,0:T(8,128)(2,1)S(1)}, bf16[4,256,256]{2,1,0:T(8,128)(2,1)S(1)}, f32[8,128]{1,0:T(8,128)S(1)}) custom-call(s32[3]{0:T(128)S(1)} %pad_add_fusion.place.refs_0_, ...), custom_call_target="tpu_custom_call", output_to_operand_aliasing={{0}: (5, {}), {1}: (6, {}), {2}: (7, {}), {3}: (8, {})} | custom-call | flops 671088640 | bytes 6291456 | tf_op jit(solution)/shard_map/pallas_call | solution.py:79
  27.1 1.7 %collective-permute-start.14 = (bf16[4,2,128,256]{3,2,1,0:T(8,128)(2,1)S(1)}, bf16[4,2,128,256]{3,2,1,0:T(8,128)(2,1)S(1)}, u32[]{:S(2)}, u32[]{:S(2)}) collective-permute-start(bf16[4,2,128,256]{3,2,1,0:T(8,128)(2,1)S(1)} %get-tuple-element.81), channel_id=1, source_target_pairs={{0,64},{4,68},{8,72},{12,76},{16,80},{20,84},{24,88},{28,92},{1,65... | collective-permute-start | bytes 1572872 | tf_op jit(solution)/shard_map/ppermute | solution.py:62
  28.7 2.9 %collective-permute-start.15 = (bf16[4,2,128,256]{3,2,1,0:T(8,128)(2,1)S(1)}, bf16[4,2,128,256]{3,2,1,0:T(8,128)(2,1)S(1)}, u32[]{:S(2)}, u32[]{:S(2)}) collective-permute-start(bf16[4,2,128,256]{3,2,1,0:T(8,128)(2,1)S(1)} %get-tuple-element.82), channel_id=1, source_target_pairs={{0,128},{4,132},{8,136},{12,140},{16,144},{20,148},{24,152},{28,15... | collective-permute-start | bytes 1572872 | tf_op jit(solution)/shard_map/ppermute | solution.py:62
  31.6 1.3 %collective-permute-start.16 = (bf16[4,2,128,256]{3,2,1,0:T(8,128)(2,1)S(1)}, bf16[4,2,128,256]{3,2,1,0:T(8,128)(2,1)S(1)}, u32[]{:S(2)}, u32[]{:S(2)}) collective-permute-start(bf16[4,2,128,256]{3,2,1,0:T(8,128)(2,1)S(1)} %get-tuple-element.83), channel_id=1, source_target_pairs={{0,192},{4,196},{8,200},{12,204},{16,208},{20,212},{24,216},{28,22... | collective-permute-start | bytes 1572872 | tf_op jit(solution)/shard_map/ppermute | solution.py:62
  33.9 2.3 %shard_map.126 = (f32[4,256,256]{2,1,0:T(8,128)S(1)}, bf16[4,256,256]{2,1,0:T(8,128)(2,1)S(1)}, bf16[4,256,256]{2,1,0:T(8,128)(2,1)S(1)}, bf16[4,256,256]{2,1,0:T(8,128)(2,1)S(1)}, f32[8,128]{1,0:T(8,128)S(1)}) custom-call(s32[3]{0:T(128)S(1)} %pad_add_fusion.place.refs_0_, ...), custom_call_target="tpu_custom_call", output_to_operand_aliasing={{0}: (5, {}), {1}: (6, {}), {2}: (7, {}), {3}: (8, {})} | custom-call | flops 671088640 | bytes 6291456 | tf_op jit(solution)/shard_map/pallas_call | solution.py:79
  37.1 2.9 %shard_map.129 = (f32[4,256,256]{2,1,0:T(8,128)S(1)}, bf16[4,256,256]{2,1,0:T(8,128)(2,1)S(1)}, bf16[4,256,256]{2,1,0:T(8,128)(2,1)S(1)}, bf16[4,256,256]{2,1,0:T(8,128)(2,1)S(1)}, f32[8,128]{1,0:T(8,128)}) custom-call(s32[3]{0:T(128)S(1)} %pad_add_fusion.place.refs_0_, ...), custom_call_target="tpu_custom_call", output_to_operand_aliasing={{0}: (5, {}), {1}: (6, {}), {2}: (7, {}), {3}: (8, {})} | custom-call | flops 671088640 | bytes 6291456 | tf_op jit(solution)/shard_map/pallas_call | solution.py:79
  41.2 3.2 %collective-permute-done.15.refs_2_ = bf16[4,2,128,256]{3,2,1,0:T(8,128)(2,1)S(1)} collective-permute-done((bf16[4,2,128,256]{3,2,1,0:T(8,128)(2,1)S(1)}, bf16[4,2,128,256]{3,2,1,0:T(8,128)(2,1)S(1)}, u32[]{:S(2)}, u32[]{:S(2)}) %collective-permute-start.15) | collective-permute-done | bytes 524320 | tf_op jit(solution)/shard_map/ppermute | solution.py:62
  45.5 2.2 %collective-permute-start.13 = (bf16[4,256,256]{2,1,0:T(8,128)(2,1)S(1)}, bf16[4,256,256]{2,1,0:T(8,128)(2,1)S(1)}, u32[]{:S(2)}, u32[]{:S(2)}) collective-permute-start(bf16[4,256,256]{2,1,0:T(8,128)(2,1)S(1)} %get-tuple-element.79), channel_id=1, source_target_pairs={{0,1},{4,5},{8,9},{12,13},{16,17},{20,21},{24,25},{28,29},{1,2},{5... | collective-permute-start | bytes 1572872 | tf_op jit(solution)/shard_map/ppermute | solution.py:56
  50.9 4.3 %collective-permute-done.17.two = bf16[4,256,256]{2,1,0:T(8,128)(2,1)S(1)} collective-permute-done((bf16[4,256,256]{2,1,0:T(8,128)(2,1)S(1)}, bf16[4,256,256]{2,1,0:T(8,128)(2,1)S(1)}, u32[]{:S(2)}, u32[]{:S(2)}) %collective-permute-start.17) | collective-permute-done | bytes 524320 | tf_op jit(solution)/shard_map/ppermute | solution.py:56
  55.2 5.5 %collective-permute-done.13.one = bf16[4,256,256]{2,1,0:T(8,128)(2,1)S(1)} collective-permute-done((bf16[4,256,256]{2,1,0:T(8,128)(2,1)S(1)}, bf16[4,256,256]{2,1,0:T(8,128)(2,1)S(1)}, u32[]{:S(2)}, u32[]{:S(2)}) %collective-permute-start.13) | collective-permute-done | bytes 524320 | tf_op jit(solution)/shard_map/ppermute | solution.py:56
  61.5 1.7 %collective-permute-start.19 = (bf16[256,256]{1,0:T(8,128)(2,1)S(1)}, bf16[256,256]{1,0:T(8,128)(2,1)S(1)}, u32[]{:S(2)}, u32[]{:S(2)}) collective-permute-start(bf16[256,256]{1,0:T(8,128)(2,1)S(1)} %get-tuple-element.86), channel_id=1, source_target_pairs={{0,64},{4,68},{8,72},{12,76},{16,80},{20,84},{24,88},{28,92},{1,65... | collective-permute-start | bytes 393224 | tf_op jit(solution)/shard_map/ppermute | solution.py:62
  63.3 2.1 %collective-permute-start.20 = (bf16[256,256]{1,0:T(8,128)(2,1)S(1)}, bf16[256,256]{1,0:T(8,128)(2,1)S(1)}, u32[]{:S(2)}, u32[]{:S(2)}) collective-permute-start(bf16[256,256]{1,0:T(8,128)(2,1)S(1)} %get-tuple-element.87), channel_id=1, source_target_pairs={{0,128},{4,132},{8,136},{12,140},{16,144},{20,148},{24,152},{28,15... | collective-permute-start | bytes 393224 | tf_op jit(solution)/shard_map/ppermute | solution.py:62
  65.4 1.7 %collective-permute-start.21 = (bf16[256,256]{1,0:T(8,128)(2,1)S(1)}, bf16[256,256]{1,0:T(8,128)(2,1)S(1)}, u32[]{:S(2)}, u32[]{:S(2)}) collective-permute-start(bf16[256,256]{1,0:T(8,128)(2,1)S(1)} %get-tuple-element.88), channel_id=1, source_target_pairs={{0,192},{4,196},{8,200},{12,204},{16,208},{20,212},{24,216},{28,22... | collective-permute-start | bytes 393224 | tf_op jit(solution)/shard_map/ppermute | solution.py:62
  67.8 1.9 %collective-permute-done.20 = bf16[256,256]{1,0:T(8,128)(2,1)S(1)} collective-permute-done((bf16[256,256]{1,0:T(8,128)(2,1)S(1)}, bf16[256,256]{1,0:T(8,128)(2,1)S(1)}, u32[]{:S(2)}, u32[]{:S(2)}) %collective-permute-start.20) | collective-permute-done | bytes 131104 | tf_op jit(solution)/shard_map/ppermute | solution.py:62
  70.4 2.0 %collective-permute-start.22 = (bf16[256,256]{1,0:T(8,128)(2,1)S(1)}, bf16[256,256]{1,0:T(8,128)(2,1)S(1)}, u32[]{:S(2)}, u32[]{:S(2)}) collective-permute-start(bf16[256,256]{1,0:T(8,128)(2,1)S(1)} %add_convert_fusion), channel_id=1, source_target_pairs={{0,0},{4,36},{8,72},{12,108},{16,144},{20,180},{24,216},{28,252},{... | collective-permute-start | bytes 393224 | tf_op jit(solution)/shard_map/ppermute | solution.py:68
  72.4 6.4 %collective-permute-done.22.gradient = bf16[256,256]{1,0:T(8,128)(2,1)S(1)} collective-permute-done((bf16[256,256]{1,0:T(8,128)(2,1)S(1)}, bf16[256,256]{1,0:T(8,128)(2,1)S(1)}, u32[]{:S(2)}, u32[]{:S(2)}) %collective-permute-start.22) | collective-permute-done | bytes 131104 | tf_op jit(solution)/shard_map/ppermute | solution.py:68
  79.9 1.3 %collective-permute-done.23.other_weight = bf16[256,256]{1,0:T(8,128)(2,1)S(1)} collective-permute-done((bf16[256,256]{1,0:T(8,128)(2,1)S(1)}, bf16[256,256]{1,0:T(8,128)(2,1)S(1)}, u32[]{:S(2)}, u32[]{:S(2)}) %collective-permute-start.23) | collective-permute-done | bytes 131104 | tf_op jit(solution)/shard_map/ppermute | solution.py:43
  82.0 2.4 %collective-permute-start.24 = (bf16[4,128,256]{2,1,0:T(8,128)(2,1)S(1)}, bf16[4,128,256]{2,1,0:T(8,128)(2,1)S(1)}, u32[]{:S(2)}, u32[]{:S(2)}) collective-permute-start(bf16[4,128,256]{2,1,0:T(8,128)(2,1)S(1)} %get-tuple-element.95), channel_id=1, source_target_pairs={{0,3},{4,7},{8,11},{12,15},{16,19},{20,23},{24,27},{28,31},{1,0},{... | collective-permute-start | bytes 786440 | tf_op jit(solution)/shard_map/ppermute | solution.py:56
  85.4 5.8 %collective-permute-done.24.one = bf16[4,128,256]{2,1,0:T(8,128)(2,1)S(1)} collective-permute-done((bf16[4,128,256]{2,1,0:T(8,128)(2,1)S(1)}, bf16[4,128,256]{2,1,0:T(8,128)(2,1)S(1)}, u32[]{:S(2)}, u32[]{:S(2)}) %collective-permute-start.24) | collective-permute-done | bytes 262176 | tf_op jit(solution)/shard_map/ppermute | solution.py:56
  92.4 2.7 %collective-permute-done.26.three = bf16[4,128,256]{2,1,0:T(8,128)(2,1)S(1)} collective-permute-done((bf16[4,128,256]{2,1,0:T(8,128)(2,1)S(1)}, bf16[4,128,256]{2,1,0:T(8,128)(2,1)S(1)}, u32[]{:S(2)}, u32[]{:S(2)}) %collective-permute-start.26) | collective-permute-done | bytes 262176 | tf_op jit(solution)/shard_map/ppermute | solution.py:56
  95.2 8.3 %collective-permute-start.27 = (f32[128,256]{1,0:T(8,128)S(1)}, f32[128,256]{1,0:T(8,128)S(1)}, u32[]{:S(2)}, u32[]{:S(2)}) collective-permute-start(f32[128,256]{1,0:T(8,128)S(1)} %get-tuple-element.99), channel_id=1, source_target_pairs={{0,192},{4,196},{8,200},{12,204},{16,208},{20,212},{24,216},{28,22... | collective-permute-start | bytes 393224 | tf_op jit(solution)/shard_map/ppermute | solution.py:62
  104.5 3.0 %collective-permute-done.27.one = f32[128,256]{1,0:T(8,128)S(1)} collective-permute-done((f32[128,256]{1,0:T(8,128)S(1)}, f32[128,256]{1,0:T(8,128)S(1)}, u32[]{:S(2)}, u32[]{:S(2)}) %collective-permute-start.27) | collective-permute-done | bytes 131104 | tf_op jit(solution)/shard_map/ppermute | solution.py:62
  107.4 2.7 %collective-permute-done.28.two = f32[128,256]{1,0:T(8,128)S(1)} collective-permute-done((f32[128,256]{1,0:T(8,128)S(1)}, f32[128,256]{1,0:T(8,128)S(1)}, u32[]{:S(2)}, u32[]{:S(2)}) %collective-permute-start.28) | collective-permute-done | bytes 131104 | tf_op jit(solution)/shard_map/ppermute | solution.py:62
  111.1 1.9 %shard_map.136 = bf16[128,1024]{1,0:T(8,128)(2,1)} custom-call(f32[128,256]{1,0:T(8,128)S(1)} %get-tuple-element.98.own, f32[128,256]{1,0:T(8,128)S(1)} %collective-permute-done.27.one, f32[128,256]{1,0:T(8,128)S(1)} %collective-permute-done.28.two, f32[128,256]{1,0:T(8,128)S(1)} %collective-permute-done.29.three, bf16[128,1024]{1,0:T(8,128)(2,1)S(1)} %bitcast.47, ...), custom_call_target="tpu_custom_call" | custom-call | bytes 1048576 | tf_op jit(solution)/shard_map/pallas_call | solution.py:79
  (73 shorter events, 21.6 us)
Async XLA Ops:
  0.6 14.9 %collective-permute-start = (bf16[640,1024]{1,0:T(8,128)(2,1)}, bf16[640,1024]{1,0:T(8,128)(2,1)S(1)}, u32[]{:S(2)}, u32[]{:S(2)}) collective-permute-start(bf16[640,1024]{1,0:T(8,128)(2,1)} %refs_1_.9), channel_id=1, source_target_pairs={{0,32},{4,36},{8,40},{12,44},{16,48},{20,52},{24,56},{28,60},{1,33... | collective-permute-start | bytes 3932168 | tf_op jit(solution)/shard_map/ppermute | solution.py:43
  0.7 5.5 %collective-permute-start.5 = (bf16[640,256]{1,0:T(8,128)(2,1)}, bf16[640,256]{1,0:T(8,128)(2,1)S(1)}, u32[]{:S(2)}, u32[]{:S(2)}) collective-permute-start(bf16[640,256]{1,0:T(8,128)(2,1)} %refs_3_.1), channel_id=1, source_target_pairs={{0,32},{4,36},{8,40},{12,44},{16,48},{20,52},{24,56},{28,60},{1,33... | collective-permute-start | bytes 983048 | tf_op jit(solution)/shard_map/ppermute | solution.py:43
  1.2 11.1 %collective-permute-start.1 = (bf16[640,256]{1,0:T(8,128)(2,1)}, bf16[640,256]{1,0:T(8,128)(2,1)S(1)}, u32[]{:S(2)}, u32[]{:S(2)}) collective-permute-start(bf16[640,256]{1,0:T(8,128)(2,1)} %refs_3_.1), channel_id=1, source_target_pairs={{0,4},{4,8},{8,12},{12,16},{16,20},{20,24},{24,28},{28,0},{1,5},{5... | collective-permute-start | bytes 983048 | tf_op jit(solution)/shard_map/ppermute | solution.py:47
  6.2 12.5 %collective-permute-start.6 = (bf16[640,256]{1,0:T(8,128)(2,1)S(1)}, bf16[640,256]{1,0:T(8,128)(2,1)S(1)}, u32[]{:S(2)}, u32[]{:S(2)}) collective-permute-start(bf16[640,256]{1,0:T(8,128)(2,1)S(1)} %shard_map.121.refs_4_), channel_id=1, source_target_pairs={{0,4},{4,8},{8,12},{12,16},{16,20},{20,24},{24,28},{28,0},{1,5},{5... | collective-permute-start | bytes 983048 | tf_op jit(solution)/shard_map/ppermute | solution.py:47
  8.2 18.7 %collective-permute-start.10 = (bf16[4,2,128,256]{3,2,1,0:T(8,128)(2,1)S(1)}, bf16[4,2,128,256]{3,2,1,0:T(8,128)(2,1)S(1)}, u32[]{:S(2)}, u32[]{:S(2)}) collective-permute-start(bf16[4,2,128,256]{3,2,1,0:T(8,128)(2,1)S(1)} %get-tuple-element.67), channel_id=1, source_target_pairs={{0,2},{4,6},{8,10},{12,14},{16,18},{20,22},{24,26},{28,30},{1,3},{... | collective-permute-start | bytes 1572872 | tf_op jit(solution)/shard_map/ppermute | solution.py:56
  11.2 15.7 %collective-permute-start.11 = (bf16[4,2,128,256]{3,2,1,0:T(8,128)(2,1)S(1)}, bf16[4,2,128,256]{3,2,1,0:T(8,128)(2,1)S(1)}, u32[]{:S(2)}, u32[]{:S(2)}) collective-permute-start(bf16[4,2,128,256]{3,2,1,0:T(8,128)(2,1)S(1)} %get-tuple-element.68), channel_id=1, source_target_pairs={{0,3},{4,7},{8,11},{12,15},{16,19},{20,23},{24,27},{28,31},{1,0},{... | collective-permute-start | bytes 1572872 | tf_op jit(solution)/shard_map/ppermute | solution.py:56
  12.4 7.7 %collective-permute-start.2 = (bf16[640,256]{1,0:T(8,128)(2,1)S(1)}, bf16[640,256]{1,0:T(8,128)(2,1)S(1)}, u32[]{:S(2)}, u32[]{:S(2)}) collective-permute-start(bf16[640,256]{1,0:T(8,128)(2,1)S(1)} %collective-permute-done.1.refs_3_), channel_id=1, source_target_pairs={{0,4},{4,8},{8,12},{12,16},{16,20},{20,24},{24,28},{28,0},{1,5},{5... | collective-permute-start | bytes 983048 | tf_op jit(solution)/shard_map/ppermute | solution.py:47
  15.5 11.4 %collective-permute-start.9 = (bf16[4,2,128,256]{3,2,1,0:T(8,128)(2,1)S(1)}, bf16[4,2,128,256]{3,2,1,0:T(8,128)(2,1)S(1)}, u32[]{:S(2)}, u32[]{:S(2)}) collective-permute-start(bf16[4,2,128,256]{3,2,1,0:T(8,128)(2,1)S(1)} %get-tuple-element.66), channel_id=1, source_target_pairs={{0,1},{4,5},{8,9},{12,13},{16,17},{20,21},{24,25},{28,29},{1,2},{5... | collective-permute-start | bytes 1572872 | tf_op jit(solution)/shard_map/ppermute | solution.py:56
  18.8 7.2 %collective-permute-start.7 = (bf16[640,256]{1,0:T(8,128)(2,1)S(1)}, bf16[640,256]{1,0:T(8,128)(2,1)S(1)}, u32[]{:S(2)}, u32[]{:S(2)}) collective-permute-start(bf16[640,256]{1,0:T(8,128)(2,1)S(1)} %shard_map.123.refs_4_), channel_id=1, source_target_pairs={{0,4},{4,8},{8,12},{12,16},{16,20},{20,24},{24,28},{28,0},{1,5},{5... | collective-permute-start | bytes 983048 | tf_op jit(solution)/shard_map/ppermute | solution.py:47
  20.1 12.9 %collective-permute-start.3 = (bf16[640,256]{1,0:T(8,128)(2,1)S(1)}, bf16[640,256]{1,0:T(8,128)(2,1)S(1)}, u32[]{:S(2)}, u32[]{:S(2)}) collective-permute-start(bf16[640,256]{1,0:T(8,128)(2,1)S(1)} %collective-permute-done.2.refs_3_), channel_id=1, source_target_pairs={{0,4},{4,8},{8,12},{12,16},{16,20},{20,24},{24,28},{28,0},{1,5},{5... | collective-permute-start | bytes 983048 | tf_op jit(solution)/shard_map/ppermute | solution.py:47
  25.9 10.3 %collective-permute-start.8 = (bf16[640,256]{1,0:T(8,128)(2,1)S(1)}, bf16[640,256]{1,0:T(8,128)(2,1)S(1)}, u32[]{:S(2)}, u32[]{:S(2)}) collective-permute-start(bf16[640,256]{1,0:T(8,128)(2,1)S(1)} %shard_map.125.refs_4_), channel_id=1, source_target_pairs={{0,4},{4,8},{8,12},{12,16},{16,20},{20,24},{24,28},{28,0},{1,5},{5... | collective-permute-start | bytes 983048 | tf_op jit(solution)/shard_map/ppermute | solution.py:47
  27.1 14.1 %collective-permute-start.14 = (bf16[4,2,128,256]{3,2,1,0:T(8,128)(2,1)S(1)}, bf16[4,2,128,256]{3,2,1,0:T(8,128)(2,1)S(1)}, u32[]{:S(2)}, u32[]{:S(2)}) collective-permute-start(bf16[4,2,128,256]{3,2,1,0:T(8,128)(2,1)S(1)} %get-tuple-element.81), channel_id=1, source_target_pairs={{0,64},{4,68},{8,72},{12,76},{16,80},{20,84},{24,88},{28,92},{1,65... | collective-permute-start | bytes 1572872 | tf_op jit(solution)/shard_map/ppermute | solution.py:62
  28.7 15.7 %collective-permute-start.15 = (bf16[4,2,128,256]{3,2,1,0:T(8,128)(2,1)S(1)}, bf16[4,2,128,256]{3,2,1,0:T(8,128)(2,1)S(1)}, u32[]{:S(2)}, u32[]{:S(2)}) collective-permute-start(bf16[4,2,128,256]{3,2,1,0:T(8,128)(2,1)S(1)} %get-tuple-element.82), channel_id=1, source_target_pairs={{0,128},{4,132},{8,136},{12,140},{16,144},{20,148},{24,152},{28,15... | collective-permute-start | bytes 1572872 | tf_op jit(solution)/shard_map/ppermute | solution.py:62
  31.6 12.8 %collective-permute-start.16 = (bf16[4,2,128,256]{3,2,1,0:T(8,128)(2,1)S(1)}, bf16[4,2,128,256]{3,2,1,0:T(8,128)(2,1)S(1)}, u32[]{:S(2)}, u32[]{:S(2)}) collective-permute-start(bf16[4,2,128,256]{3,2,1,0:T(8,128)(2,1)S(1)} %get-tuple-element.83), channel_id=1, source_target_pairs={{0,192},{4,196},{8,200},{12,204},{16,208},{20,212},{24,216},{28,22... | collective-permute-start | bytes 1572872 | tf_op jit(solution)/shard_map/ppermute | solution.py:62
  33.0 7.0 %collective-permute-start.4 = (bf16[640,256]{1,0:T(8,128)(2,1)S(1)}, bf16[640,256]{1,0:T(8,128)(2,1)S(1)}, u32[]{:S(2)}, u32[]{:S(2)}) collective-permute-start(bf16[640,256]{1,0:T(8,128)(2,1)S(1)} %collective-permute-done.3.refs_3_), channel_id=1, source_target_pairs={{32,60},{36,32},{40,36},{44,40},{48,44},{52,48},{56,52},{60,56},{3... | collective-permute-start | bytes 983048 | tf_op jit(solution)/shard_map/ppermute | solution.py:52
  36.2 3.8 %collective-permute-start.12 = (bf16[640,256]{1,0:T(8,128)(2,1)S(1)}, bf16[640,256]{1,0:T(8,128)(2,1)S(1)}, u32[]{:S(2)}, u32[]{:S(2)}) collective-permute-start(bf16[640,256]{1,0:T(8,128)(2,1)S(1)} %shard_map.128.refs_4_), channel_id=1, source_target_pairs={{32,60},{36,32},{40,36},{44,40},{48,44},{52,48},{56,52},{60,56},{3... | collective-permute-start | bytes 983048 | tf_op jit(solution)/shard_map/ppermute | solution.py:52
  44.4 10.8 %collective-permute-start.17 = (bf16[4,256,256]{2,1,0:T(8,128)(2,1)S(1)}, bf16[4,256,256]{2,1,0:T(8,128)(2,1)S(1)}, u32[]{:S(2)}, u32[]{:S(2)}) collective-permute-start(bf16[4,256,256]{2,1,0:T(8,128)(2,1)S(1)} %shard_map.131), channel_id=1, source_target_pairs={{0,2},{4,6},{8,10},{12,14},{16,18},{20,22},{24,26},{28,30},{1,3},{... | collective-permute-start | bytes 1572872 | tf_op jit(solution)/shard_map/ppermute | solution.py:56
  45.5 15.3 %collective-permute-start.13 = (bf16[4,256,256]{2,1,0:T(8,128)(2,1)S(1)}, bf16[4,256,256]{2,1,0:T(8,128)(2,1)S(1)}, u32[]{:S(2)}, u32[]{:S(2)}) collective-permute-start(bf16[4,256,256]{2,1,0:T(8,128)(2,1)S(1)} %get-tuple-element.79), channel_id=1, source_target_pairs={{0,1},{4,5},{8,9},{12,13},{16,17},{20,21},{24,25},{28,29},{1,2},{5... | collective-permute-start | bytes 1572872 | tf_op jit(solution)/shard_map/ppermute | solution.py:56
  47.6 13.1 %collective-permute-start.18 = (bf16[4,256,256]{2,1,0:T(8,128)(2,1)S(1)}, bf16[4,256,256]{2,1,0:T(8,128)(2,1)S(1)}, u32[]{:S(2)}, u32[]{:S(2)}) collective-permute-start(bf16[4,256,256]{2,1,0:T(8,128)(2,1)S(1)} %get-tuple-element.84), channel_id=1, source_target_pairs={{0,3},{4,7},{8,11},{12,15},{16,19},{20,23},{24,27},{28,31},{1,0},{... | collective-permute-start | bytes 1572872 | tf_op jit(solution)/shard_map/ppermute | solution.py:56
  50.9 27.9 %copy-start.4 = (f32[256,256]{1,0:T(8,128)S(1)}, f32[256,256]{1,0:T(8,128)}, u32[]{:S(2)}) copy-start(f32[256,256]{1,0:T(8,128)} %master.1) | copy-start | bytes 786436
  50.9 27.9 %copy-start.5 = (bf16[256,256]{1,0:T(8,128)(2,1)S(1)}, bf16[256,256]{1,0:T(8,128)(2,1)}, u32[]{:S(2)}) copy-start(bf16[256,256]{1,0:T(8,128)(2,1)} %first_moment.1) | copy-start | bytes 393220
  61.5 6.3 %collective-permute-start.19 = (bf16[256,256]{1,0:T(8,128)(2,1)S(1)}, bf16[256,256]{1,0:T(8,128)(2,1)S(1)}, u32[]{:S(2)}, u32[]{:S(2)}) collective-permute-start(bf16[256,256]{1,0:T(8,128)(2,1)S(1)} %get-tuple-element.86), channel_id=1, source_target_pairs={{0,64},{4,68},{8,72},{12,76},{16,80},{20,84},{24,88},{28,92},{1,65... | collective-permute-start | bytes 393224 | tf_op jit(solution)/shard_map/ppermute | solution.py:62
  63.3 6.5 %collective-permute-start.20 = (bf16[256,256]{1,0:T(8,128)(2,1)S(1)}, bf16[256,256]{1,0:T(8,128)(2,1)S(1)}, u32[]{:S(2)}, u32[]{:S(2)}) collective-permute-start(bf16[256,256]{1,0:T(8,128)(2,1)S(1)} %get-tuple-element.87), channel_id=1, source_target_pairs={{0,128},{4,132},{8,136},{12,140},{16,144},{20,148},{24,152},{28,15... | collective-permute-start | bytes 393224 | tf_op jit(solution)/shard_map/ppermute | solution.py:62
  65.4 5.0 %collective-permute-start.21 = (bf16[256,256]{1,0:T(8,128)(2,1)S(1)}, bf16[256,256]{1,0:T(8,128)(2,1)S(1)}, u32[]{:S(2)}, u32[]{:S(2)}) collective-permute-start(bf16[256,256]{1,0:T(8,128)(2,1)S(1)} %get-tuple-element.88), channel_id=1, source_target_pairs={{0,192},{4,196},{8,200},{12,204},{16,208},{20,212},{24,216},{28,22... | collective-permute-start | bytes 393224 | tf_op jit(solution)/shard_map/ppermute | solution.py:62
  70.4 8.4 %collective-permute-start.22 = (bf16[256,256]{1,0:T(8,128)(2,1)S(1)}, bf16[256,256]{1,0:T(8,128)(2,1)S(1)}, u32[]{:S(2)}, u32[]{:S(2)}) collective-permute-start(bf16[256,256]{1,0:T(8,128)(2,1)S(1)} %add_convert_fusion), channel_id=1, source_target_pairs={{0,0},{4,36},{8,72},{12,108},{16,144},{20,180},{24,216},{28,252},{... | collective-permute-start | bytes 393224 | tf_op jit(solution)/shard_map/ppermute | solution.py:68
  79.9 1.3 %collective-permute-start.23 = (bf16[256,256]{1,0:T(8,128)(2,1)S(1)}, bf16[256,256]{1,0:T(8,128)(2,1)S(1)}, u32[]{:S(2)}, u32[]{:S(2)}) collective-permute-start(bf16[256,256]{1,0:T(8,128)(2,1)S(1)} %get-tuple-element.92.weight), channel_id=1, source_target_pairs={{0,32},{4,36},{8,40},{12,44},{16,48},{20,52},{24,56},{28,60},{1,33... | collective-permute-start | bytes 393224 | tf_op jit(solution)/shard_map/ppermute | solution.py:43
  82.0 9.2 %collective-permute-start.24 = (bf16[4,128,256]{2,1,0:T(8,128)(2,1)S(1)}, bf16[4,128,256]{2,1,0:T(8,128)(2,1)S(1)}, u32[]{:S(2)}, u32[]{:S(2)}) collective-permute-start(bf16[4,128,256]{2,1,0:T(8,128)(2,1)S(1)} %get-tuple-element.95), channel_id=1, source_target_pairs={{0,3},{4,7},{8,11},{12,15},{16,19},{20,23},{24,27},{28,31},{1,0},{... | collective-permute-start | bytes 786440 | tf_op jit(solution)/shard_map/ppermute | solution.py:56
  84.4 8.0 %collective-permute-start.25 = (bf16[4,128,256]{2,1,0:T(8,128)(2,1)S(1)}, bf16[4,128,256]{2,1,0:T(8,128)(2,1)S(1)}, u32[]{:S(2)}, u32[]{:S(2)}) collective-permute-start(bf16[4,128,256]{2,1,0:T(8,128)(2,1)S(1)} %get-tuple-element.96), channel_id=1, source_target_pairs={{0,2},{4,6},{8,10},{12,14},{16,18},{20,22},{24,26},{28,30},{1,3},{... | collective-permute-start | bytes 786440 | tf_op jit(solution)/shard_map/ppermute | solution.py:56
  84.7 10.4 %collective-permute-start.26 = (bf16[4,128,256]{2,1,0:T(8,128)(2,1)S(1)}, bf16[4,128,256]{2,1,0:T(8,128)(2,1)S(1)}, u32[]{:S(2)}, u32[]{:S(2)}) collective-permute-start(bf16[4,128,256]{2,1,0:T(8,128)(2,1)S(1)} %get-tuple-element.97), channel_id=1, source_target_pairs={{0,1},{4,5},{8,9},{12,13},{16,17},{20,21},{24,25},{28,29},{1,2},{5... | collective-permute-start | bytes 786440 | tf_op jit(solution)/shard_map/ppermute | solution.py:56
  95.2 12.2 %collective-permute-start.27 = (f32[128,256]{1,0:T(8,128)S(1)}, f32[128,256]{1,0:T(8,128)S(1)}, u32[]{:S(2)}, u32[]{:S(2)}) collective-permute-start(f32[128,256]{1,0:T(8,128)S(1)} %get-tuple-element.99), channel_id=1, source_target_pairs={{0,192},{4,196},{8,200},{12,204},{16,208},{20,212},{24,216},{28,22... | collective-permute-start | bytes 393224 | tf_op jit(solution)/shard_map/ppermute | solution.py:62
  103.5 6.6 %collective-permute-start.28 = (f32[128,256]{1,0:T(8,128)S(1)}, f32[128,256]{1,0:T(8,128)S(1)}, u32[]{:S(2)}, u32[]{:S(2)}) collective-permute-start(f32[128,256]{1,0:T(8,128)S(1)} %get-tuple-element.100), channel_id=1, source_target_pairs={{0,128},{4,132},{8,136},{12,140},{16,144},{20,148},{24,152},{28,15... | collective-permute-start | bytes 393224 | tf_op jit(solution)/shard_map/ppermute | solution.py:62
  103.5 7.6 %collective-permute-start.29 = (f32[128,256]{1,0:T(8,128)S(1)}, f32[128,256]{1,0:T(8,128)S(1)}, u32[]{:S(2)}, u32[]{:S(2)}) collective-permute-start(f32[128,256]{1,0:T(8,128)S(1)} %get-tuple-element.101), channel_id=1, source_target_pairs={{0,64},{4,68},{8,72},{12,76},{16,80},{20,84},{24,88},{28,92},{1,65... | collective-permute-start | bytes 393224 | tf_op jit(solution)/shard_map/ppermute | solution.py:62
  (7 other events, 71.7 us)
where the time goes:
time: 113 us
  starting transfers between devices  49.2 us (44%)
  waiting for transfers between devices  41.6 us (37%)
  Pallas kernels  17.2 us (15%)
  local copies, waits for them, and re-layouts  2 us (2%)
  matrix products  1.39 us (1%)
    ppermute x9, starting transfers between devices, shift_second(): lax.ppermute(a, AXES, pairs_of(lambda y, k, x, z: (y + d, k, x, z) if k =...  20.7 us
    ppermute x9, waiting for transfers between devices, shift_first(): lax.ppermute(a, AXES, pairs_of(lambda y, k, x, z: (y, k, x + d, z) if k =...  19.5 us
    pallas_call x17, Pallas kernels, call(): pl.pallas_call(kernel, out_shape=out, in_specs=in_specs, out_specs=out_sp...  17.2 us
    ppermute x9, waiting for transfers between devices, shift_second(): lax.ppermute(a, AXES, pairs_of(lambda y, k, x, z: (y + d, k, x, z) if k =...  13.1 us
    ppermute x9, starting transfers between devices, shift_first(): lax.ppermute(a, AXES, pairs_of(lambda y, k, x, z: (y, k, x + d, z) if k =...  12.7 us
    ppermute x6, starting transfers between devices, pass_on(): lax.ppermute(a, AXES, pairs_of(lambda y, k, x, z: (y, k, x, z + 1 - 2 * k)))  11.6 us
    ppermute x1, waiting for transfers between devices, to_owner(): lax.ppermute(a, AXES, pairs_of(lambda y, k, x, z: (z // 2, z % 2, x, z +...  6.36 us
  transfers between devices with their start and end apart: 30, of which 16 were waited for; matrix products, arithmetic and copies ran while one was open for 2% of the time, Pallas kernels for 11%

commit v1 on v0

--- a/solution.py
+++ b/solution.py
@@ -113,28 +113,49 @@
     slot = jnp.where(k == 0, step, 4 - step)
     token[...] = jnp.zeros_like(token)
 
-    @pl.when((slot >= 0) & (slot < 4))
-    def _():
+    def turn():
         turned[0] = block[...].T
         turned[1] = other_block[...].T
+
+    def tile(a):
+        at = pl.ds(pl.multiple_of(a * 256, 256), 256)
+        return jnp.dot(turned[0], own_x[:, at], preferred_element_type=f32) + jnp.dot(
+            turned[1], other_x[:, at], preferred_element_type=f32
+        )
+
+    if step == 4:
+
+        @pl.when(k == 1)
+        def _():
+            turn()
+            for d, out in enumerate((keep, one, two, three)):
+
+                @pl.when(lax.rem(p + d, 4) == 0)
+                def _():
+                    for a in range(4):
+                        out[a] = tile(a).astype(out.dtype)
+
+        return
+
+    @pl.when(slot < 4)
+    def _():
+        turn()
 
         def one_tile(i, carry):
             a = jnp.where(k == 0, lax.rem(p + i, 4), i)
             d = jnp.where(k == 0, i, lax.rem(slot - p + 4, 4))
             index = jnp.where(k == 0, slot, i)
-            at = pl.ds(pl.multiple_of(a * 256, 256), 256)
-            tile = jnp.dot(turned[0], own_x[:, at], preferred_element_type=f32)
-            tile = tile + jnp.dot(turned[1], other_x[:, at], preferred_element_type=f32)
+            result = tile(a)
 
             @pl.when(d == 0)
             def _():
-                keep[index] = tile
+                keep[index] = result
 
             for m, out in ((1, one), (2, two), (3, three)):
 
                 @pl.when(d == m)
                 def _():
-                    out[index] = tile.astype(bf16)
+                    out[index] = result.astype(bf16)
 
             return carry
 
@@ -210,11 +231,12 @@
     for n, out in enumerate(outs):
         out[...] = (
             keep[n] + one[n].astype(f32) + two[n].astype(f32) + three[n].astype(f32)
-        )
+        ).astype(out.dtype)
 
 
 def finish_kernel(own, one, two, three, queries, peak, mass, past, out):
-    fresh = (own[...] + one[...] + two[...] + three[...]).astype(bf16)
+    fresh = own[...] + one[...].astype(f32) + two[...].astype(f32) + three[...].astype(f32)
+    fresh = fresh.astype(bf16)
     n = fresh.shape[0]
     rows = n // 4
     group = HEADS // KVH
@@ -235,9 +257,10 @@
     weight = jnp.where(seen, jnp.exp(scores - top), 0.0)
     fade = jnp.exp(before - top)
     total = mass * fade + jnp.sum(weight, axis=1, keepdims=True)
-    probs = (weight / total).astype(bf16)
+    share = 1.0 / total
+    probs = (weight * share).astype(bf16)
     result = jnp.dot(probs, values, preferred_element_type=f32)
-    result = (result + past[...] * (fade / total)).astype(bf16)
+    result = (result + past[...] * (fade * share)).astype(bf16)
     for g in range(group):
         out[:, g * HD : g * HD + HD] = result[g * n : g * n + n]
 
@@ -342,7 +365,7 @@
 
     keep, one, two, three = buffers
     peak, mass, past = past_part(queries, kv_cache, cache_lengths)
-    two = after_all(two, *states[1:])
+    three = after_all(three, *states[1:])
     one, two, three = shift_first(one, 1), shift_first(two, 2), shift_first(three, 3)
     square, narrow = shape((256, 256), f32), shape((256, 256), bf16)
     own, one, two, three = call(
@@ -377,10 +400,10 @@
         moved=4 << 20,
     )
     one, two, three = shift_first(one, -1), shift_first(two, -2), shift_first(three, -3)
-    result = shape((count, 256), f32)
+    result, sent = shape((count, 256), f32), shape((count, 256), bf16)
     own, one, two, three = call(
         gather_kernel,
-        (result,) * 4,
+        (result, sent, sent, sent),
         (keep, one, two, three),
         [VMEM] * 4,
         [VMEM] * 4,

time: 113 us -> 111 us (0.982)
  starting transfers between devices: 49.2 us -> 47 us
    ppermute x9, waiting for transfers between devices: 19.5 us -> 21.2 us  [shift_first(): lax.ppermute(a, AXES, pairs_of(lambda y, k, x, z: (y, k, x + d, z) if k =...]
    ppermute x9, starting transfers between devices: 12.7 us -> 11 us  [shift_first(): lax.ppermute(a, AXES, pairs_of(lambda y, k, x, z: (y, k, x + d, z) if k =...]
    ppermute x9, waiting for transfers between devices: 13.1 us -> 11.7 us  [shift_second(): lax.ppermute(a, AXES, pairs_of(lambda y, k, x, z: (y + d, k, x, z) if k =...]
where the time goes in v1:
time: 111 us
  starting transfers between devices  47 us (42%)
  waiting for transfers between devices  42 us (38%)
  Pallas kernels  17.2 us (15%)
  local copies, waits for them, and re-layouts  2 us (2%)
  matrix products  1.39 us (1%)
    ppermute x9, waiting for transfers between devices, shift_first(): lax.ppermute(a, AXES, pairs_of(lambda y, k, x, z: (y, k, x + d, z) if k =...  21.2 us
    ppermute x9, starting transfers between devices, shift_second(): lax.ppermute(a, AXES, pairs_of(lambda y, k, x, z: (y + d, k, x, z) if k =...  20.3 us
    pallas_call x17, Pallas kernels, call(): pl.pallas_call(kernel, out_shape=out, in_specs=in_specs, out_specs=out_sp...  17.2 us
    ppermute x9, waiting for transfers between devices, shift_second(): lax.ppermute(a, AXES, pairs_of(lambda y, k, x, z: (y + d, k, x, z) if k =...  11.7 us
    ppermute x6, starting transfers between devices, pass_on(): lax.ppermute(a, AXES, pairs_of(lambda y, k, x, z: (y, k, x, z + 1 - 2 * k)))  11.6 us
    ppermute x9, starting transfers between devices, shift_first(): lax.ppermute(a, AXES, pairs_of(lambda y, k, x, z: (y, k, x + d, z) if k =...  11 us
    ppermute x1, waiting for transfers between devices, to_owner(): lax.ppermute(a, AXES, pairs_of(lambda y, k, x, z: (z // 2, z % 2, x, z +...  6.47 us
  transfers between devices with their start and end apart: 30, of which 16 were waited for; matrix products, arithmetic and copies ran while one was open for 2% of the time, Pallas kernels for 11%

profile of v1, /device:TPU:32, one launch (start us, length us, event | category | flops | bytes accessed | tf_op | source)
XLA Modules:
  0.0 111.1 jit_solution(8966158189509977874)
XLA Ops:
  1.2 1.9 %collective-permute-start.1 = (bf16[640,256]{1,0:T(8,128)(2,1)}, bf16[640,256]{1,0:T(8,128)(2,1)S(1)}, u32[]{:S(2)}, u32[]{:S(2)}) collective-permute-start(bf16[640,256]{1,0:T(8,128)(2,1)} %refs_3_.1), channel_id=1, source_target_pairs={{0,4},{4,8},{8,12},{12,16},{16,20},{20,24},{24,28},{28,0},{1,5},{5... | collective-permute-start | bytes 983048 | tf_op jit(solution)/shard_map/ppermute | solution.py:47
  3.2 1.6 %copy-done.1 = bf16[4,32,8192]{2,1,0:T(8,128)(2,1)S(1)} copy-done((bf16[4,32,8192]{2,1,0:T(8,128)(2,1)S(1)}, bf16[4,32,8192]{2,1,0:T(8,128)(2,1)}, u32[]{:S(2)}) %copy-start.1) | copy-done | bytes 2097176
  4.8 1.4 %shard_map.120 = (bf16[4,2,128,256]{3,2,1,0:T(8,128)(2,1)S(1)}, bf16[4,2,128,256]{3,2,1,0:T(8,128)(2,1)S(1)}, bf16[4,2,128,256]{3,2,1,0:T(8,128)(2,1)S(1)}, bf16...) custom-call(s32[3]{0:T(128)S(1)} %pad_add_fusion.place.refs_0_, bf16[128,8192]{1,0:T(8,128)(2,1)S(1)} %bitcast.45), custom_call_target="tpu_custom_call" | custom-call | bytes 4194304 | tf_op jit(solution)/shard_map/pallas_call | solution.py:79
  6.2 2.0 %collective-permute-start.6 = (bf16[640,256]{1,0:T(8,128)(2,1)S(1)}, bf16[640,256]{1,0:T(8,128)(2,1)S(1)}, u32[]{:S(2)}, u32[]{:S(2)}) collective-permute-start(bf16[640,256]{1,0:T(8,128)(2,1)S(1)} %shard_map.121.refs_4_), channel_id=1, source_target_pairs={{0,4},{4,8},{8,12},{12,16},{16,20},{20,24},{24,28},{28,0},{1,5},{5... | collective-permute-start | bytes 983048 | tf_op jit(solution)/shard_map/ppermute | solution.py:47
  8.2 3.0 %collective-permute-start.10 = (bf16[4,2,128,256]{3,2,1,0:T(8,128)(2,1)S(1)}, bf16[4,2,128,256]{3,2,1,0:T(8,128)(2,1)S(1)}, u32[]{:S(2)}, u32[]{:S(2)}) collective-permute-start(bf16[4,2,128,256]{3,2,1,0:T(8,128)(2,1)S(1)} %get-tuple-element.67), channel_id=1, source_target_pairs={{0,2},{4,6},{8,10},{12,14},{16,18},{20,22},{24,26},{28,30},{1,3},{... | collective-permute-start | bytes 1572872 | tf_op jit(solution)/shard_map/ppermute | solution.py:56
  12.4 3.1 %collective-permute-start.2 = (bf16[640,256]{1,0:T(8,128)(2,1)S(1)}, bf16[640,256]{1,0:T(8,128)(2,1)S(1)}, u32[]{:S(2)}, u32[]{:S(2)}) collective-permute-start(bf16[640,256]{1,0:T(8,128)(2,1)S(1)} %collective-permute-done.1.refs_3_), channel_id=1, source_target_pairs={{0,4},{4,8},{8,12},{12,16},{16,20},{20,24},{24,28},{28,0},{1,5},{5... | collective-permute-start | bytes 983048 | tf_op jit(solution)/shard_map/ppermute | solution.py:47
  16.4 2.3 %shard_map.122 = (f32[4,256,256]{2,1,0:T(8,128)S(1)}, bf16[4,256,256]{2,1,0:T(8,128)(2,1)S(1)}, bf16[4,256,256]{2,1,0:T(8,128)(2,1)S(1)}, bf16[4,256,256]{2,1,0:T(8,128)(2,1)S(1)}, f32[8,128]{1,0:T(8,128)S(1)}) custom-call(s32[3]{0:T(128)S(1)} %pad_add_fusion.place.refs_0_, bf16[640,1024]{1,0:T(8,128)(2,1)S(1)} %copy-done, ...), custom_call_target="tpu_custom_call" | custom-call | flops 671088640 | bytes 6291456 | tf_op jit(solution)/shard_map/pallas_call | solution.py:79
  20.1 2.5 %collective-permute-start.3 = (bf16[640,256]{1,0:T(8,128)(2,1)S(1)}, bf16[640,256]{1,0:T(8,128)(2,1)S(1)}, u32[]{:S(2)}, u32[]{:S(2)}) collective-permute-start(bf16[640,256]{1,0:T(8,128)(2,1)S(1)} %collective-permute-done.2.refs_3_), channel_id=1, source_target_pairs={{0,4},{4,8},{8,12},{12,16},{16,20},{20,24},{24,28},{28,0},{1,5},{5... | collective-permute-start | bytes 983048 | tf_op jit(solution)/shard_map/ppermute | solution.py:47
  22.6 2.3 %shard_map.124 = (f32[4,256,256]{2,1,0:T(8,128)S(1)}, bf16[4,256,256]{2,1,0:T(8,128)(2,1)S(1)}, bf16[4,256,256]{2,1,0:T(8,128)(2,1)S(1)}, bf16[4,256,256]{2,1,0:T(8,128)(2,1)S(1)}, f32[8,128]{1,0:T(8,128)S(1)}) custom-call(s32[3]{0:T(128)S(1)} %pad_add_fusion.place.refs_0_, ...), custom_call_target="tpu_custom_call", output_to_operand_aliasing={{0}: (5, {}), {1}: (6, {}), {2}: (7, {}), {3}: (8, {})} | custom-call | flops 671088640 | bytes 6291456 | tf_op jit(solution)/shard_map/pallas_call | solution.py:79
  27.1 1.7 %collective-permute-start.15 = (bf16[4,2,128,256]{3,2,1,0:T(8,128)(2,1)S(1)}, bf16[4,2,128,256]{3,2,1,0:T(8,128)(2,1)S(1)}, u32[]{:S(2)}, u32[]{:S(2)}) collective-permute-start(bf16[4,2,128,256]{3,2,1,0:T(8,128)(2,1)S(1)} %get-tuple-element.82), channel_id=1, source_target_pairs={{0,64},{4,68},{8,72},{12,76},{16,80},{20,84},{24,88},{28,92},{1,65... | collective-permute-start | bytes 1572872 | tf_op jit(solution)/shard_map/ppermute | solution.py:62
  28.7 2.9 %collective-permute-start.16 = (bf16[4,2,128,256]{3,2,1,0:T(8,128)(2,1)S(1)}, bf16[4,2,128,256]{3,2,1,0:T(8,128)(2,1)S(1)}, u32[]{:S(2)}, u32[]{:S(2)}) collective-permute-start(bf16[4,2,128,256]{3,2,1,0:T(8,128)(2,1)S(1)} %get-tuple-element.83), channel_id=1, source_target_pairs={{0,128},{4,132},{8,136},{12,140},{16,144},{20,148},{24,152},{28,15... | collective-permute-start | bytes 1572872 | tf_op jit(solution)/shard_map/ppermute | solution.py:62
  33.9 2.3 %shard_map.126 = (f32[4,256,256]{2,1,0:T(8,128)S(1)}, bf16[4,256,256]{2,1,0:T(8,128)(2,1)S(1)}, bf16[4,256,256]{2,1,0:T(8,128)(2,1)S(1)}, bf16[4,256,256]{2,1,0:T(8,128)(2,1)S(1)}, f32[8,128]{1,0:T(8,128)S(1)}) custom-call(s32[3]{0:T(128)S(1)} %pad_add_fusion.place.refs_0_, ...), custom_call_target="tpu_custom_call", output_to_operand_aliasing={{0}: (5, {}), {1}: (6, {}), {2}: (7, {}), {3}: (8, {})} | custom-call | flops 671088640 | bytes 6291456 | tf_op jit(solution)/shard_map/pallas_call | solution.py:79
  37.1 2.9 %shard_map.129 = (f32[4,256,256]{2,1,0:T(8,128)S(1)}, bf16[4,256,256]{2,1,0:T(8,128)(2,1)S(1)}, bf16[4,256,256]{2,1,0:T(8,128)(2,1)S(1)}, bf16[4,256,256]{2,1,0:T(8,128)(2,1)S(1)}, f32[8,128]{1,0:T(8,128)}) custom-call(s32[3]{0:T(128)S(1)} %pad_add_fusion.place.refs_0_, ...), custom_call_target="tpu_custom_call", output_to_operand_aliasing={{0}: (5, {}), {1}: (6, {}), {2}: (7, {}), {3}: (8, {})} | custom-call | flops 671088640 | bytes 6291456 | tf_op jit(solution)/shard_map/pallas_call | solution.py:79
  41.2 3.2 %collective-permute-done.16.refs_2_ = bf16[4,2,128,256]{3,2,1,0:T(8,128)(2,1)S(1)} collective-permute-done((bf16[4,2,128,256]{3,2,1,0:T(8,128)(2,1)S(1)}, bf16[4,2,128,256]{3,2,1,0:T(8,128)(2,1)S(1)}, u32[]{:S(2)}, u32[]{:S(2)}) %collective-permute-start.16) | collective-permute-done | bytes 524320 | tf_op jit(solution)/shard_map/ppermute | solution.py:62
  44.4 2.3 %collective-permute-start.18 = (bf16[4,256,256]{2,1,0:T(8,128)(2,1)S(1)}, bf16[4,256,256]{2,1,0:T(8,128)(2,1)S(1)}, u32[]{:S(2)}, u32[]{:S(2)}) collective-permute-start(bf16[4,256,256]{2,1,0:T(8,128)(2,1)S(1)} %shard_map.131), channel_id=1, source_target_pairs={{0,3},{4,7},{8,11},{12,15},{16,19},{20,23},{24,27},{28,31},{1,0},{... | collective-permute-start | bytes 1572872 | tf_op jit(solution)/shard_map/ppermute | solution.py:56
  46.8 1.5 %collective-permute-start.14 = (bf16[4,256,256]{2,1,0:T(8,128)(2,1)S(1)}, bf16[4,256,256]{2,1,0:T(8,128)(2,1)S(1)}, u32[]{:S(2)}, u32[]{:S(2)}) collective-permute-start(bf16[4,256,256]{2,1,0:T(8,128)(2,1)S(1)} %get-tuple-element.80), channel_id=1, source_target_pairs={{0,2},{4,6},{8,10},{12,14},{16,18},{20,22},{24,26},{28,30},{1,3},{... | collective-permute-start | bytes 1572872 | tf_op jit(solution)/shard_map/ppermute | solution.py:56
  50.5 8.6 %collective-permute-done.18.three = bf16[4,256,256]{2,1,0:T(8,128)(2,1)S(1)} collective-permute-done((bf16[4,256,256]{2,1,0:T(8,128)(2,1)S(1)}, bf16[4,256,256]{2,1,0:T(8,128)(2,1)S(1)}, u32[]{:S(2)}, u32[]{:S(2)}) %collective-permute-start.18) | collective-permute-done | bytes 524320 | tf_op jit(solution)/shard_map/ppermute | solution.py:56
  59.1 3.7 %collective-permute-done.13.one = bf16[4,256,256]{2,1,0:T(8,128)(2,1)S(1)} collective-permute-done((bf16[4,256,256]{2,1,0:T(8,128)(2,1)S(1)}, bf16[4,256,256]{2,1,0:T(8,128)(2,1)S(1)}, u32[]{:S(2)}, u32[]{:S(2)}) %collective-permute-start.13) | collective-permute-done | bytes 524320 | tf_op jit(solution)/shard_map/ppermute | solution.py:56
  63.6 1.7 %collective-permute-start.19 = (bf16[256,256]{1,0:T(8,128)(2,1)S(1)}, bf16[256,256]{1,0:T(8,128)(2,1)S(1)}, u32[]{:S(2)}, u32[]{:S(2)}) collective-permute-start(bf16[256,256]{1,0:T(8,128)(2,1)S(1)} %get-tuple-element.86), channel_id=1, source_target_pairs={{0,64},{4,68},{8,72},{12,76},{16,80},{20,84},{24,88},{28,92},{1,65... | collective-permute-start | bytes 393224 | tf_op jit(solution)/shard_map/ppermute | solution.py:62
  65.3 2.1 %collective-permute-start.20 = (bf16[256,256]{1,0:T(8,128)(2,1)S(1)}, bf16[256,256]{1,0:T(8,128)(2,1)S(1)}, u32[]{:S(2)}, u32[]{:S(2)}) collective-permute-start(bf16[256,256]{1,0:T(8,128)(2,1)S(1)} %get-tuple-element.87), channel_id=1, source_target_pairs={{0,128},{4,132},{8,136},{12,140},{16,144},{20,148},{24,152},{28,15... | collective-permute-start | bytes 393224 | tf_op jit(solution)/shard_map/ppermute | solution.py:62
  67.4 1.7 %collective-permute-start.21 = (bf16[256,256]{1,0:T(8,128)(2,1)S(1)}, bf16[256,256]{1,0:T(8,128)(2,1)S(1)}, u32[]{:S(2)}, u32[]{:S(2)}) collective-permute-start(bf16[256,256]{1,0:T(8,128)(2,1)S(1)} %get-tuple-element.88), channel_id=1, source_target_pairs={{0,192},{4,196},{8,200},{12,204},{16,208},{20,212},{24,216},{28,22... | collective-permute-start | bytes 393224 | tf_op jit(solution)/shard_map/ppermute | solution.py:62
  69.8 1.9 %collective-permute-done.20 = bf16[256,256]{1,0:T(8,128)(2,1)S(1)} collective-permute-done((bf16[256,256]{1,0:T(8,128)(2,1)S(1)}, bf16[256,256]{1,0:T(8,128)(2,1)S(1)}, u32[]{:S(2)}, u32[]{:S(2)}) %collective-permute-start.20) | collective-permute-done | bytes 131104 | tf_op jit(solution)/shard_map/ppermute | solution.py:62
  72.5 1.9 %collective-permute-start.22 = (bf16[256,256]{1,0:T(8,128)(2,1)S(1)}, bf16[256,256]{1,0:T(8,128)(2,1)S(1)}, u32[]{:S(2)}, u32[]{:S(2)}) collective-permute-start(bf16[256,256]{1,0:T(8,128)(2,1)S(1)} %add_convert_fusion), channel_id=1, source_target_pairs={{0,0},{4,36},{8,72},{12,108},{16,144},{20,180},{24,216},{28,252},{... | collective-permute-start | bytes 393224 | tf_op jit(solution)/shard_map/ppermute | solution.py:68
  74.4 6.5 %collective-permute-done.22.gradient = bf16[256,256]{1,0:T(8,128)(2,1)S(1)} collective-permute-done((bf16[256,256]{1,0:T(8,128)(2,1)S(1)}, bf16[256,256]{1,0:T(8,128)(2,1)S(1)}, u32[]{:S(2)}, u32[]{:S(2)}) %collective-permute-start.22) | collective-permute-done | bytes 131104 | tf_op jit(solution)/shard_map/ppermute | solution.py:68
  84.7 1.4 %collective-permute-start.26 = (bf16[4,128,256]{2,1,0:T(8,128)(2,1)S(1)}, bf16[4,128,256]{2,1,0:T(8,128)(2,1)S(1)}, u32[]{:S(2)}, u32[]{:S(2)}) collective-permute-start(bf16[4,128,256]{2,1,0:T(8,128)(2,1)S(1)} %get-tuple-element.97), channel_id=1, source_target_pairs={{0,1},{4,5},{8,9},{12,13},{16,17},{20,21},{24,25},{28,29},{1,2},{5... | collective-permute-start | bytes 786440 | tf_op jit(solution)/shard_map/ppermute | solution.py:56
  86.1 4.3 %collective-permute-done.24.one = bf16[4,128,256]{2,1,0:T(8,128)(2,1)S(1)} collective-permute-done((bf16[4,128,256]{2,1,0:T(8,128)(2,1)S(1)}, bf16[4,128,256]{2,1,0:T(8,128)(2,1)S(1)}, u32[]{:S(2)}, u32[]{:S(2)}) %collective-permute-start.24) | collective-permute-done | bytes 262176 | tf_op jit(solution)/shard_map/ppermute | solution.py:56
  90.5 1.9 %collective-permute-done.25.two = bf16[4,128,256]{2,1,0:T(8,128)(2,1)S(1)} collective-permute-done((bf16[4,128,256]{2,1,0:T(8,128)(2,1)S(1)}, bf16[4,128,256]{2,1,0:T(8,128)(2,1)S(1)}, u32[]{:S(2)}, u32[]{:S(2)}) %collective-permute-start.25) | collective-permute-done | bytes 262176 | tf_op jit(solution)/shard_map/ppermute | solution.py:56
  92.4 2.7 %collective-permute-done.26.three = bf16[4,128,256]{2,1,0:T(8,128)(2,1)S(1)} collective-permute-done((bf16[4,128,256]{2,1,0:T(8,128)(2,1)S(1)}, bf16[4,128,256]{2,1,0:T(8,128)(2,1)S(1)}, u32[]{:S(2)}, u32[]{:S(2)}) %collective-permute-start.26) | collective-permute-done | bytes 262176 | tf_op jit(solution)/shard_map/ppermute | solution.py:56
  95.2 7.8 %collective-permute-start.27 = (bf16[128,256]{1,0:T(8,128)(2,1)S(1)}, bf16[128,256]{1,0:T(8,128)(2,1)S(1)}, u32[]{:S(2)}, u32[]{:S(2)}) collective-permute-start(bf16[128,256]{1,0:T(8,128)(2,1)S(1)} %get-tuple-element.99), channel_id=1, source_target_pairs={{0,192},{4,196},{8,200},{12,204},{16,208},{20,212},{24,216},{28,22... | collective-permute-start | bytes 196616 | tf_op jit(solution)/shard_map/ppermute | solution.py:62
  104.0 1.6 %collective-permute-done.27.one = bf16[128,256]{1,0:T(8,128)(2,1)S(1)} collective-permute-done((bf16[128,256]{1,0:T(8,128)(2,1)S(1)}, bf16[128,256]{1,0:T(8,128)(2,1)S(1)}, u32[]{:S(2)}, u32[]{:S(2)}) %collective-permute-start.27) | collective-permute-done | bytes 65568 | tf_op jit(solution)/shard_map/ppermute | solution.py:62
  105.6 3.4 %collective-permute-done.28.two = bf16[128,256]{1,0:T(8,128)(2,1)S(1)} collective-permute-done((bf16[128,256]{1,0:T(8,128)(2,1)S(1)}, bf16[128,256]{1,0:T(8,128)(2,1)S(1)}, u32[]{:S(2)}, u32[]{:S(2)}) %collective-permute-start.28) | collective-permute-done | bytes 65568 | tf_op jit(solution)/shard_map/ppermute | solution.py:62
  109.3 1.9 %shard_map.136 = bf16[128,1024]{1,0:T(8,128)(2,1)} custom-call(f32[128,256]{1,0:T(8,128)S(1)} %get-tuple-element.98.own, bf16[128,256]{1,0:T(8,128)(2,1)S(1)} %collective-permute-done.27.one, bf16[128,256]{1,0:T(8,128)(2,1)S(1)} %collective-permute-done.28.two, bf16[128,256]{1,0:T(8,128)(2,1)S(1)} %collective-permute-done.29.three, ...), custom_call_target="tpu_custom_call" | custom-call | bytes 1048576 | tf_op jit(solution)/shard_map/pallas_call | solution.py:79
  (73 shorter events, 20.0 us)
Async XLA Ops:
  0.6 14.9 %collective-permute-start = (bf16[640,1024]{1,0:T(8,128)(2,1)}, bf16[640,1024]{1,0:T(8,128)(2,1)S(1)}, u32[]{:S(2)}, u32[]{:S(2)}) collective-permute-start(bf16[640,1024]{1,0:T(8,128)(2,1)} %refs_1_.9), channel_id=1, source_target_pairs={{0,32},{4,36},{8,40},{12,44},{16,48},{20,52},{24,56},{28,60},{1,33... | collective-permute-start | bytes 3932168 | tf_op jit(solution)/shard_map/ppermute | solution.py:43
  0.7 5.5 %collective-permute-start.5 = (bf16[640,256]{1,0:T(8,128)(2,1)}, bf16[640,256]{1,0:T(8,128)(2,1)S(1)}, u32[]{:S(2)}, u32[]{:S(2)}) collective-permute-start(bf16[640,256]{1,0:T(8,128)(2,1)} %refs_3_.1), channel_id=1, source_target_pairs={{0,32},{4,36},{8,40},{12,44},{16,48},{20,52},{24,56},{28,60},{1,33... | collective-permute-start | bytes 983048 | tf_op jit(solution)/shard_map/ppermute | solution.py:43
  1.2 11.1 %collective-permute-start.1 = (bf16[640,256]{1,0:T(8,128)(2,1)}, bf16[640,256]{1,0:T(8,128)(2,1)S(1)}, u32[]{:S(2)}, u32[]{:S(2)}) collective-permute-start(bf16[640,256]{1,0:T(8,128)(2,1)} %refs_3_.1), channel_id=1, source_target_pairs={{0,4},{4,8},{8,12},{12,16},{16,20},{20,24},{24,28},{28,0},{1,5},{5... | collective-permute-start | bytes 983048 | tf_op jit(solution)/shard_map/ppermute | solution.py:47
  6.2 12.5 %collective-permute-start.6 = (bf16[640,256]{1,0:T(8,128)(2,1)S(1)}, bf16[640,256]{1,0:T(8,128)(2,1)S(1)}, u32[]{:S(2)}, u32[]{:S(2)}) collective-permute-start(bf16[640,256]{1,0:T(8,128)(2,1)S(1)} %shard_map.121.refs_4_), channel_id=1, source_target_pairs={{0,4},{4,8},{8,12},{12,16},{16,20},{20,24},{24,28},{28,0},{1,5},{5... | collective-permute-start | bytes 983048 | tf_op jit(solution)/shard_map/ppermute | solution.py:47
  8.2 18.7 %collective-permute-start.10 = (bf16[4,2,128,256]{3,2,1,0:T(8,128)(2,1)S(1)}, bf16[4,2,128,256]{3,2,1,0:T(8,128)(2,1)S(1)}, u32[]{:S(2)}, u32[]{:S(2)}) collective-permute-start(bf16[4,2,128,256]{3,2,1,0:T(8,128)(2,1)S(1)} %get-tuple-element.67), channel_id=1, source_target_pairs={{0,2},{4,6},{8,10},{12,14},{16,18},{20,22},{24,26},{28,30},{1,3},{... | collective-permute-start | bytes 1572872 | tf_op jit(solution)/shard_map/ppermute | solution.py:56
  11.2 15.7 %collective-permute-start.11 = (bf16[4,2,128,256]{3,2,1,0:T(8,128)(2,1)S(1)}, bf16[4,2,128,256]{3,2,1,0:T(8,128)(2,1)S(1)}, u32[]{:S(2)}, u32[]{:S(2)}) collective-permute-start(bf16[4,2,128,256]{3,2,1,0:T(8,128)(2,1)S(1)} %get-tuple-element.68), channel_id=1, source_target_pairs={{0,3},{4,7},{8,11},{12,15},{16,19},{20,23},{24,27},{28,31},{1,0},{... | collective-permute-start | bytes 1572872 | tf_op jit(solution)/shard_map/ppermute | solution.py:56
  12.4 7.7 %collective-permute-start.2 = (bf16[640,256]{1,0:T(8,128)(2,1)S(1)}, bf16[640,256]{1,0:T(8,128)(2,1)S(1)}, u32[]{:S(2)}, u32[]{:S(2)}) collective-permute-start(bf16[640,256]{1,0:T(8,128)(2,1)S(1)} %collective-permute-done.1.refs_3_), channel_id=1, source_target_pairs={{0,4},{4,8},{8,12},{12,16},{16,20},{20,24},{24,28},{28,0},{1,5},{5... | collective-permute-start | bytes 983048 | tf_op jit(solution)/shard_map/ppermute | solution.py:47
  15.5 11.4 %collective-permute-start.9 = (bf16[4,2,128,256]{3,2,1,0:T(8,128)(2,1)S(1)}, bf16[4,2,128,256]{3,2,1,0:T(8,128)(2,1)S(1)}, u32[]{:S(2)}, u32[]{:S(2)}) collective-permute-start(bf16[4,2,128,256]{3,2,1,0:T(8,128)(2,1)S(1)} %get-tuple-element.66), channel_id=1, source_target_pairs={{0,1},{4,5},{8,9},{12,13},{16,17},{20,21},{24,25},{28,29},{1,2},{5... | collective-permute-start | bytes 1572872 | tf_op jit(solution)/shard_map/ppermute | solution.py:56
  18.8 7.2 %collective-permute-start.7 = (bf16[640,256]{1,0:T(8,128)(2,1)S(1)}, bf16[640,256]{1,0:T(8,128)(2,1)S(1)}, u32[]{:S(2)}, u32[]{:S(2)}) collective-permute-start(bf16[640,256]{1,0:T(8,128)(2,1)S(1)} %shard_map.123.refs_4_), channel_id=1, source_target_pairs={{0,4},{4,8},{8,12},{12,16},{16,20},{20,24},{24,28},{28,0},{1,5},{5... | collective-permute-start | bytes 983048 | tf_op jit(solution)/shard_map/ppermute | solution.py:47
  20.1 12.9 %collective-permute-start.3 = (bf16[640,256]{1,0:T(8,128)(2,1)S(1)}, bf16[640,256]{1,0:T(8,128)(2,1)S(1)}, u32[]{:S(2)}, u32[]{:S(2)}) collective-permute-start(bf16[640,256]{1,0:T(8,128)(2,1)S(1)} %collective-permute-done.2.refs_3_), channel_id=1, source_target_pairs={{0,4},{4,8},{8,12},{12,16},{16,20},{20,24},{24,28},{28,0},{1,5},{5... | collective-permute-start | bytes 983048 | tf_op jit(solution)/shard_map/ppermute | solution.py:47
  25.9 10.3 %collective-permute-start.8 = (bf16[640,256]{1,0:T(8,128)(2,1)S(1)}, bf16[640,256]{1,0:T(8,128)(2,1)S(1)}, u32[]{:S(2)}, u32[]{:S(2)}) collective-permute-start(bf16[640,256]{1,0:T(8,128)(2,1)S(1)} %shard_map.125.refs_4_), channel_id=1, source_target_pairs={{0,4},{4,8},{8,12},{12,16},{16,20},{20,24},{24,28},{28,0},{1,5},{5... | collective-permute-start | bytes 983048 | tf_op jit(solution)/shard_map/ppermute | solution.py:47
  27.1 14.1 %collective-permute-start.15 = (bf16[4,2,128,256]{3,2,1,0:T(8,128)(2,1)S(1)}, bf16[4,2,128,256]{3,2,1,0:T(8,128)(2,1)S(1)}, u32[]{:S(2)}, u32[]{:S(2)}) collective-permute-start(bf16[4,2,128,256]{3,2,1,0:T(8,128)(2,1)S(1)} %get-tuple-element.82), channel_id=1, source_target_pairs={{0,64},{4,68},{8,72},{12,76},{16,80},{20,84},{24,88},{28,92},{1,65... | collective-permute-start | bytes 1572872 | tf_op jit(solution)/shard_map/ppermute | solution.py:62
  28.7 15.7 %collective-permute-start.16 = (bf16[4,2,128,256]{3,2,1,0:T(8,128)(2,1)S(1)}, bf16[4,2,128,256]{3,2,1,0:T(8,128)(2,1)S(1)}, u32[]{:S(2)}, u32[]{:S(2)}) collective-permute-start(bf16[4,2,128,256]{3,2,1,0:T(8,128)(2,1)S(1)} %get-tuple-element.83), channel_id=1, source_target_pairs={{0,128},{4,132},{8,136},{12,140},{16,144},{20,148},{24,152},{28,15... | collective-permute-start | bytes 1572872 | tf_op jit(solution)/shard_map/ppermute | solution.py:62
  31.6 12.8 %collective-permute-start.17 = (bf16[4,2,128,256]{3,2,1,0:T(8,128)(2,1)S(1)}, bf16[4,2,128,256]{3,2,1,0:T(8,128)(2,1)S(1)}, u32[]{:S(2)}, u32[]{:S(2)}) collective-permute-start(bf16[4,2,128,256]{3,2,1,0:T(8,128)(2,1)S(1)} %get-tuple-element.84), channel_id=1, source_target_pairs={{0,192},{4,196},{8,200},{12,204},{16,208},{20,212},{24,216},{28,22... | collective-permute-start | bytes 1572872 | tf_op jit(solution)/shard_map/ppermute | solution.py:62
  33.0 7.0 %collective-permute-start.4 = (bf16[640,256]{1,0:T(8,128)(2,1)S(1)}, bf16[640,256]{1,0:T(8,128)(2,1)S(1)}, u32[]{:S(2)}, u32[]{:S(2)}) collective-permute-start(bf16[640,256]{1,0:T(8,128)(2,1)S(1)} %collective-permute-done.3.refs_3_), channel_id=1, source_target_pairs={{32,60},{36,32},{40,36},{44,40},{48,44},{52,48},{56,52},{60,56},{3... | collective-permute-start | bytes 983048 | tf_op jit(solution)/shard_map/ppermute | solution.py:52
  36.2 3.8 %collective-permute-start.12 = (bf16[640,256]{1,0:T(8,128)(2,1)S(1)}, bf16[640,256]{1,0:T(8,128)(2,1)S(1)}, u32[]{:S(2)}, u32[]{:S(2)}) collective-permute-start(bf16[640,256]{1,0:T(8,128)(2,1)S(1)} %shard_map.128.refs_4_), channel_id=1, source_target_pairs={{32,60},{36,32},{40,36},{44,40},{48,44},{52,48},{56,52},{60,56},{3... | collective-permute-start | bytes 983048 | tf_op jit(solution)/shard_map/ppermute | solution.py:52
  44.4 14.7 %collective-permute-start.18 = (bf16[4,256,256]{2,1,0:T(8,128)(2,1)S(1)}, bf16[4,256,256]{2,1,0:T(8,128)(2,1)S(1)}, u32[]{:S(2)}, u32[]{:S(2)}) collective-permute-start(bf16[4,256,256]{2,1,0:T(8,128)(2,1)S(1)} %shard_map.131), channel_id=1, source_target_pairs={{0,3},{4,7},{8,11},{12,15},{16,19},{20,23},{24,27},{28,31},{1,0},{... | collective-permute-start | bytes 1572872 | tf_op jit(solution)/shard_map/ppermute | solution.py:56
  46.8 16.0 %collective-permute-start.13 = (bf16[4,256,256]{2,1,0:T(8,128)(2,1)S(1)}, bf16[4,256,256]{2,1,0:T(8,128)(2,1)S(1)}, u32[]{:S(2)}, u32[]{:S(2)}) collective-permute-start(bf16[4,256,256]{2,1,0:T(8,128)(2,1)S(1)} %get-tuple-element.79), channel_id=1, source_target_pairs={{0,1},{4,5},{8,9},{12,13},{16,17},{20,21},{24,25},{28,29},{1,2},{5... | collective-permute-start | bytes 1572872 | tf_op jit(solution)/shard_map/ppermute | solution.py:56
  46.8 16.0 %collective-permute-start.14 = (bf16[4,256,256]{2,1,0:T(8,128)(2,1)S(1)}, bf16[4,256,256]{2,1,0:T(8,128)(2,1)S(1)}, u32[]{:S(2)}, u32[]{:S(2)}) collective-permute-start(bf16[4,256,256]{2,1,0:T(8,128)(2,1)S(1)} %get-tuple-element.80), channel_id=1, source_target_pairs={{0,2},{4,6},{8,10},{12,14},{16,18},{20,22},{24,26},{28,30},{1,3},{... | collective-permute-start | bytes 1572872 | tf_op jit(solution)/shard_map/ppermute | solution.py:56
  50.5 30.4 %copy-start.4 = (f32[256,256]{1,0:T(8,128)S(1)}, f32[256,256]{1,0:T(8,128)}, u32[]{:S(2)}) copy-start(f32[256,256]{1,0:T(8,128)} %master.1) | copy-start | bytes 786436
  50.5 30.3 %copy-start.5 = (bf16[256,256]{1,0:T(8,128)(2,1)S(1)}, bf16[256,256]{1,0:T(8,128)(2,1)}, u32[]{:S(2)}) copy-start(bf16[256,256]{1,0:T(8,128)(2,1)} %first_moment.1) | copy-start | bytes 393220
  63.6 6.3 %collective-permute-start.19 = (bf16[256,256]{1,0:T(8,128)(2,1)S(1)}, bf16[256,256]{1,0:T(8,128)(2,1)S(1)}, u32[]{:S(2)}, u32[]{:S(2)}) collective-permute-start(bf16[256,256]{1,0:T(8,128)(2,1)S(1)} %get-tuple-element.86), channel_id=1, source_target_pairs={{0,64},{4,68},{8,72},{12,76},{16,80},{20,84},{24,88},{28,92},{1,65... | collective-permute-start | bytes 393224 | tf_op jit(solution)/shard_map/ppermute | solution.py:62
  65.3 6.5 %collective-permute-start.20 = (bf16[256,256]{1,0:T(8,128)(2,1)S(1)}, bf16[256,256]{1,0:T(8,128)(2,1)S(1)}, u32[]{:S(2)}, u32[]{:S(2)}) collective-permute-start(bf16[256,256]{1,0:T(8,128)(2,1)S(1)} %get-tuple-element.87), channel_id=1, source_target_pairs={{0,128},{4,132},{8,136},{12,140},{16,144},{20,148},{24,152},{28,15... | collective-permute-start | bytes 393224 | tf_op jit(solution)/shard_map/ppermute | solution.py:62
  67.4 5.0 %collective-permute-start.21 = (bf16[256,256]{1,0:T(8,128)(2,1)S(1)}, bf16[256,256]{1,0:T(8,128)(2,1)S(1)}, u32[]{:S(2)}, u32[]{:S(2)}) collective-permute-start(bf16[256,256]{1,0:T(8,128)(2,1)S(1)} %get-tuple-element.88), channel_id=1, source_target_pairs={{0,192},{4,196},{8,200},{12,204},{16,208},{20,212},{24,216},{28,22... | collective-permute-start | bytes 393224 | tf_op jit(solution)/shard_map/ppermute | solution.py:62
  72.5 8.4 %collective-permute-start.22 = (bf16[256,256]{1,0:T(8,128)(2,1)S(1)}, bf16[256,256]{1,0:T(8,128)(2,1)S(1)}, u32[]{:S(2)}, u32[]{:S(2)}) collective-permute-start(bf16[256,256]{1,0:T(8,128)(2,1)S(1)} %add_convert_fusion), channel_id=1, source_target_pairs={{0,0},{4,36},{8,72},{12,108},{16,144},{20,180},{24,216},{28,252},{... | collective-permute-start | bytes 393224 | tf_op jit(solution)/shard_map/ppermute | solution.py:68
  81.9 1.3 %collective-permute-start.23 = (bf16[256,256]{1,0:T(8,128)(2,1)S(1)}, bf16[256,256]{1,0:T(8,128)(2,1)S(1)}, u32[]{:S(2)}, u32[]{:S(2)}) collective-permute-start(bf16[256,256]{1,0:T(8,128)(2,1)S(1)} %get-tuple-element.92.weight), channel_id=1, source_target_pairs={{0,32},{4,36},{8,40},{12,44},{16,48},{20,52},{24,56},{28,60},{1,33... | collective-permute-start | bytes 393224 | tf_op jit(solution)/shard_map/ppermute | solution.py:43
  84.0 6.4 %collective-permute-start.24 = (bf16[4,128,256]{2,1,0:T(8,128)(2,1)S(1)}, bf16[4,128,256]{2,1,0:T(8,128)(2,1)S(1)}, u32[]{:S(2)}, u32[]{:S(2)}) collective-permute-start(bf16[4,128,256]{2,1,0:T(8,128)(2,1)S(1)} %get-tuple-element.95), channel_id=1, source_target_pairs={{0,3},{4,7},{8,11},{12,15},{16,19},{20,23},{24,27},{28,31},{1,0},{... | collective-permute-start | bytes 786440 | tf_op jit(solution)/shard_map/ppermute | solution.py:56
  84.1 8.3 %collective-permute-start.25 = (bf16[4,128,256]{2,1,0:T(8,128)(2,1)S(1)}, bf16[4,128,256]{2,1,0:T(8,128)(2,1)S(1)}, u32[]{:S(2)}, u32[]{:S(2)}) collective-permute-start(bf16[4,128,256]{2,1,0:T(8,128)(2,1)S(1)} %get-tuple-element.96), channel_id=1, source_target_pairs={{0,2},{4,6},{8,10},{12,14},{16,18},{20,22},{24,26},{28,30},{1,3},{... | collective-permute-start | bytes 786440 | tf_op jit(solution)/shard_map/ppermute | solution.py:56
  84.7 10.4 %collective-permute-start.26 = (bf16[4,128,256]{2,1,0:T(8,128)(2,1)S(1)}, bf16[4,128,256]{2,1,0:T(8,128)(2,1)S(1)}, u32[]{:S(2)}, u32[]{:S(2)}) collective-permute-start(bf16[4,128,256]{2,1,0:T(8,128)(2,1)S(1)} %get-tuple-element.97), channel_id=1, source_target_pairs={{0,1},{4,5},{8,9},{12,13},{16,17},{20,21},{24,25},{28,29},{1,2},{5... | collective-permute-start | bytes 786440 | tf_op jit(solution)/shard_map/ppermute | solution.py:56
  95.2 10.4 %collective-permute-start.27 = (bf16[128,256]{1,0:T(8,128)(2,1)S(1)}, bf16[128,256]{1,0:T(8,128)(2,1)S(1)}, u32[]{:S(2)}, u32[]{:S(2)}) collective-permute-start(bf16[128,256]{1,0:T(8,128)(2,1)S(1)} %get-tuple-element.99), channel_id=1, source_target_pairs={{0,192},{4,196},{8,200},{12,204},{16,208},{20,212},{24,216},{28,22... | collective-permute-start | bytes 196616 | tf_op jit(solution)/shard_map/ppermute | solution.py:62
  103.1 5.9 %collective-permute-start.28 = (bf16[128,256]{1,0:T(8,128)(2,1)S(1)}, bf16[128,256]{1,0:T(8,128)(2,1)S(1)}, u32[]{:S(2)}, u32[]{:S(2)}) collective-permute-start(bf16[128,256]{1,0:T(8,128)(2,1)S(1)} %get-tuple-element.100), channel_id=1, source_target_pairs={{0,128},{4,132},{8,136},{12,140},{16,144},{20,148},{24,152},{28,15... | collective-permute-start | bytes 196616 | tf_op jit(solution)/shard_map/ppermute | solution.py:62
  103.1 6.2 %collective-permute-start.29 = (bf16[128,256]{1,0:T(8,128)(2,1)S(1)}, bf16[128,256]{1,0:T(8,128)(2,1)S(1)}, u32[]{:S(2)}, u32[]{:S(2)}) collective-permute-start(bf16[128,256]{1,0:T(8,128)(2,1)S(1)} %get-tuple-element.101), channel_id=1, source_target_pairs={{0,64},{4,68},{8,72},{12,76},{16,80},{20,84},{24,88},{28,92},{1,65... | collective-permute-start | bytes 196616 | tf_op jit(solution)/shard_map/ppermute | solution.py:62
  (7 other events, 73.8 us)

commit v2 on v1

--- a/solution.py
+++ b/solution.py
@@ -110,7 +110,6 @@
     place, own_x, other_x, block, other_block = refs[:5]
     keep, one, two, three, token, turned = refs[-6:]
     k, p = place[0], place[1]
-    slot = jnp.where(k == 0, step, 4 - step)
     token[...] = jnp.zeros_like(token)
 
     def turn():
@@ -137,29 +136,26 @@
 
         return
 
-    @pl.when(slot < 4)
+    @pl.when(k == 0)
     def _():
         turn()
-
-        def one_tile(i, carry):
-            a = jnp.where(k == 0, lax.rem(p + i, 4), i)
-            d = jnp.where(k == 0, i, lax.rem(slot - p + 4, 4))
-            index = jnp.where(k == 0, slot, i)
-            result = tile(a)
-
-            @pl.when(d == 0)
-            def _():
-                keep[index] = result
-
-            for m, out in ((1, one), (2, two), (3, three)):
-
-                @pl.when(d == m)
+        for d, out in enumerate((keep, one, two, three)):
+            out[step] = tile(lax.rem(p + d, 4)).astype(out.dtype)
+
+    if step > 0:
+
+        @pl.when(k == 1)
+        def _():
+            turn()
+            for d, out in enumerate((keep, one, two, three)):
+
+                @pl.when(lax.rem(p + d, 4) == 4 - step)
                 def _():
-                    out[index] = result.astype(bf16)
-
-            return carry
-
-        lax.fori_loop(0, 4, one_tile, 0)
+                    def one_tile(a, carry):
+                        out[a] = tile(a).astype(out.dtype)
+                        return carry
+
+                    lax.fori_loop(0, 4, one_tile, 0)
 
 
 def middle_kernel(place, keep, one, two, three, *refs):
@@ -201,7 +197,7 @@
                 at = pl.multiple_of(((2 * y + core) * 4 + x) * 256, 256)
                 copies.append(
                     pltpu.make_async_copy(
-                        states.at[:, pl.ds(at, 256)], sends[m].at[n, i], sems.at[len(copies)]
+                        states.at[:, pl.ds(at, 256)], sends[n].at[m, i], sems.at[len(copies)]
                     )
                 )
                 copies[-1].start()
@@ -210,28 +206,15 @@
         copy.wait()
 
 
-def regroup_kernel(*refs):
-    came, sends, token = refs[:4], refs[4:8], refs[8]
-    token[...] = jnp.zeros_like(token)
-    for n in range(4):
+def project_kernel(*refs):
+    weights, states, outs = refs[:4], refs[4:8], refs[8:]
+    for n, out in enumerate(outs):
+        total = None
         for m in range(4):
-            sends[n][m] = came[m][n]
-
-
-def project_kernel(weight, other_weight, *refs):
-    states, sends = refs[:4], refs[4:]
-    for m, out in enumerate(sends):
-        for n in range(4):
-            term = jnp.dot(states[n][m, 0], weight[...], preferred_element_type=f32)
-            term = term + jnp.dot(states[n][m, 1], other_weight[...], preferred_element_type=f32)
-            out[n] = term.astype(out.dtype)
-
-
-def gather_kernel(keep, one, two, three, *outs):
-    for n, out in enumerate(outs):
-        out[...] = (
-            keep[n] + one[n].astype(f32) + two[n].astype(f32) + three[n].astype(f32)
-        ).astype(out.dtype)
+            for i in range(2):
+                term = jnp.dot(states[n][m, i], weights[m][i], preferred_element_type=f32)
+                total = term if total is None else total + term
+        out[...] = total.astype(out.dtype)
 
 
 def finish_kernel(own, one, two, three, queries, peak, mass, past, out):
@@ -243,24 +226,24 @@
     line = lax.broadcasted_iota(jnp.int32, (n, n), 0)
     lane = lax.broadcasted_iota(jnp.int32, (n, n), 1)
     seen = (lax.rem(line, rows) == lax.rem(lane, rows)) & (lane <= line)
-    seen = jnp.concatenate([seen.astype(f32)] * group, axis=0) > 0.5
+    unseen = jnp.where(seen, 0.0, -1e30)
     scale = 1.0 / math.sqrt(HD)
     keys, values = fresh[:, :HD], fresh[:, HD:]
     stack = jnp.concatenate([queries[:, g * HD : g * HD + HD] for g in range(group)], axis=0)
     scores = lax.dot_general(
         stack, keys, (((1,), (1,)), ((), ())), preferred_element_type=f32
     )
-    scores = jnp.where(seen, scores * scale, -1e30)
-    before = jnp.concatenate([peak[:, g : g + 1] for g in range(group)], axis=0)
-    mass = jnp.concatenate([mass[:, g : g + 1] for g in range(group)], axis=0)
-    top = jnp.maximum(before, jnp.max(scores, axis=1, keepdims=True))
-    weight = jnp.where(seen, jnp.exp(scores - top), 0.0)
+    scores = scores.reshape(group, n, n) * scale + unseen[None]
+    before = jnp.stack([peak[:, g : g + 1] for g in range(group)])
+    mass = jnp.stack([mass[:, g : g + 1] for g in range(group)])
+    top = jnp.maximum(before, jnp.max(scores, axis=2, keepdims=True))
+    weight = jnp.exp(scores - top)
     fade = jnp.exp(before - top)
-    total = mass * fade + jnp.sum(weight, axis=1, keepdims=True)
-    share = 1.0 / total
-    probs = (weight * share).astype(bf16)
+    share = 1.0 / (mass * fade + jnp.sum(weight, axis=2, keepdims=True))
+    probs = (weight * share).astype(bf16).reshape(group * n, n)
     result = jnp.dot(probs, values, preferred_element_type=f32)
-    result = (result + past[...] * (fade * share)).astype(bf16)
+    old = past[...].reshape(group, n, HD) * (fade * share)
+    result = (result + old.reshape(group * n, HD)).astype(bf16)
     for g in range(group):
         out[:, g * HD : g * HD + HD] = result[g * n : g * n + n]
 
@@ -339,22 +322,13 @@
         moved=4 << 20,
     )
     other_block = after_all(other_block, packed)
-    came = [sends[0]] + [shift_first(sends[d], d) for d in (1, 2, 3)]
-    *sends, regrouped = call(
-        regroup_kernel,
-        (shape(group, bf16),) * 4 + (shape((8, 128), f32),),
-        tuple(came),
-        [VMEM] * 4,
-        [VMEM] * 5,
-        moved=4 << 20,
-    )
     states = [sends[0]] + [shift_second(sends[d], d) for d in (1, 2, 3)]
 
     tokens = []
     arrived = (block, other_block)
     for step in range(5):
         if 0 < step < 4:
-            awaited = (tokens[-1], regrouped) if step == 3 else (tokens[-1],)
+            awaited = (tokens[-1], *states[1:]) if step == 3 else (tokens[-1],)
             arrived = (arrived[0], after_all(arrived[1], *awaited))
         if step < 4:
             send = pass_on if step < 3 else pass_last
@@ -365,7 +339,6 @@
 
     keep, one, two, three = buffers
     peak, mass, past = past_part(queries, kv_cache, cache_lengths)
-    three = after_all(three, *states[1:])
     one, two, three = shift_first(one, 1), shift_first(two, 2), shift_first(three, 3)
     square, narrow = shape((256, 256), f32), shape((256, 256), bf16)
     own, one, two, three = call(
@@ -389,25 +362,17 @@
         moved=1 << 20,
     )
 
-    part = (4, count, 256)
-    keep, one, two, three = call(
+    pair = jnp.stack([weight, swap_core(weight)])
+    line = [pair, shift_first(pair, -1), shift_first(pair, 2), shift_first(pair, 1)]
+    result, sent = shape((count, 256), f32), shape((count, 256), bf16)
+    own, one, two, three = call(
         project_kernel,
-        (shape(part, f32),) + (shape(part, bf16),) * 3,
-        (weight, swap_core(weight), *states),
-        [VMEM] * 6,
+        (result, sent, sent, sent),
+        (*line, *states),
+        [VMEM] * 8,
         [VMEM] * 4,
         flops=2 * 16 * count * 512 * 256,
         moved=4 << 20,
-    )
-    one, two, three = shift_first(one, -1), shift_first(two, -2), shift_first(three, -3)
-    result, sent = shape((count, 256), f32), shape((count, 256), bf16)
-    own, one, two, three = call(
-        gather_kernel,
-        (result, sent, sent, sent),
-        (keep, one, two, three),
-        [VMEM] * 4,
-        [VMEM] * 4,
-        moved=2 << 20,
     )
     one, two, three = shift_second(one, -1), shift_second(two, -2), shift_second(three, -3)
     attended = call(

time: 111 us -> 107 us (0.964)
  waiting for transfers between devices: 42 us -> 36.5 us
  starting transfers between devices: 47 us -> 51.3 us
  Pallas kernels: 17.2 us -> 14.1 us
    ppermute x1, starting transfers between devices: 1.92 us -> 5.44 us  [to_owner(): lax.ppermute(a, AXES, pairs_of(lambda y, k, x, z: (z // 2, z % 2, x, z +...]
    pallas_call x17 -> x14, Pallas kernels: 17.2 us -> 14.1 us  [call(): pl.pallas_call(kernel, out_shape=out, in_specs=in_specs, out_specs=out_sp...]
    ppermute x9 -> x6, waiting for transfers between devices: 21.2 us -> 18.7 us  [shift_first(): lax.ppermute(a, AXES, pairs_of(lambda y, k, x, z: (y, k, x + d, z) if k =...]
    ppermute x6, starting transfers between devices: 11.6 us -> 14.1 us  [pass_on(): lax.ppermute(a, AXES, pairs_of(lambda y, k, x, z: (y, k, x, z + 1 - 2 * k)))]
    ppermute x9, waiting for transfers between devices: 11.7 us -> 9.69 us  [shift_second(): lax.ppermute(a, AXES, pairs_of(lambda y, k, x, z: (y + d, k, x, z) if k =...]
    ppermute x9 -> x6, starting transfers between devices: 11 us -> 9.44 us  [shift_first(): lax.ppermute(a, AXES, pairs_of(lambda y, k, x, z: (y, k, x + d, z) if k =...]
    ppermute x1, waiting for transfers between devices: 6.47 us -> 5.24 us  [to_owner(): lax.ppermute(a, AXES, pairs_of(lambda y, k, x, z: (z // 2, z % 2, x, z +...]
  transfers between devices with their start and end apart: 30 -> 27, of which waited for: 16 -> 16; matrix products, arithmetic and copies ran while one was open for 2% -> 2% of each run, Pallas kernels for 11% -> 8%
where the time goes in v2:
time: 107 us
  starting transfers between devices  51.3 us (48%)
  waiting for transfers between devices  36.5 us (34%)
  Pallas kernels  14.1 us (13%)
  local copies, waits for them, and re-layouts  2 us (2%)
  matrix products  1.35 us (1%)
    ppermute x9, starting transfers between devices, shift_second(): lax.ppermute(a, AXES, pairs_of(lambda y, k, x, z: (y + d, k, x, z) if k =...  20.4 us
    ppermute x6, waiting for transfers between devices, shift_first(): lax.ppermute(a, AXES, pairs_of(lambda y, k, x, z: (y, k, x + d, z) if k =...  18.7 us
    pallas_call x14, Pallas kernels, call(): pl.pallas_call(kernel, out_shape=out, in_specs=in_specs, out_specs=out_sp...  14.1 us
    ppermute x6, starting transfers between devices, pass_on(): lax.ppermute(a, AXES, pairs_of(lambda y, k, x, z: (y, k, x, z + 1 - 2 * k)))  14.1 us
    ppermute x9, waiting for transfers between devices, shift_second(): lax.ppermute(a, AXES, pairs_of(lambda y, k, x, z: (y + d, k, x, z) if k =...  9.69 us
    ppermute x6, starting transfers between devices, shift_first(): lax.ppermute(a, AXES, pairs_of(lambda y, k, x, z: (y, k, x + d, z) if k =...  9.44 us
    ppermute x1, starting transfers between devices, to_owner(): lax.ppermute(a, AXES, pairs_of(lambda y, k, x, z: (z // 2, z % 2, x, z +...  5.44 us
    ppermute x1, waiting for transfers between devices, to_owner(): lax.ppermute(a, AXES, pairs_of(lambda y, k, x, z: (z // 2, z % 2, x, z +...  5.24 us
  transfers between devices with their start and end apart: 27, of which 16 were waited for; matrix products, arithmetic and copies ran while one was open for 2% of the time, Pallas kernels for 8%

profile of v2, /device:TPU:32, one launch (start us, length us, event | category | flops | bytes accessed | tf_op | source)
XLA Modules:
  0.0 106.9 jit_solution(5467199894120525422)
XLA Ops:
  1.2 1.9 %collective-permute-start.1 = (bf16[640,256]{1,0:T(8,128)(2,1)}, bf16[640,256]{1,0:T(8,128)(2,1)S(1)}, u32[]{:S(2)}, u32[]{:S(2)}) collective-permute-start(bf16[640,256]{1,0:T(8,128)(2,1)} %refs_3_.1), channel_id=1, source_target_pairs={{0,4},{4,8},{8,12},{12,16},{16,20},{20,24},{24,28},{28,0},{1,5},{5... | collective-permute-start | bytes 983048 | tf_op jit(solution)/shard_map/ppermute | solution.py:47
  3.2 1.6 %copy-done.1 = bf16[4,32,8192]{2,1,0:T(8,128)(2,1)S(1)} copy-done((bf16[4,32,8192]{2,1,0:T(8,128)(2,1)S(1)}, bf16[4,32,8192]{2,1,0:T(8,128)(2,1)}, u32[]{:S(2)}) %copy-start.1) | copy-done | bytes 2097176
  4.8 1.4 %shard_map.120 = (bf16[4,2,128,256]{3,2,1,0:T(8,128)(2,1)S(1)}, bf16[4,2,128,256]{3,2,1,0:T(8,128)(2,1)S(1)}, bf16[4,2,128,256]{3,2,1,0:T(8,128)(2,1)S(1)}, bf16...) custom-call(s32[3]{0:T(128)S(1)} %pad_add_fusion.place.refs_0_, bf16[128,8192]{1,0:T(8,128)(2,1)S(1)} %bitcast.47), custom_call_target="tpu_custom_call" | custom-call | bytes 4194304 | tf_op jit(solution)/shard_map/pallas_call | solution.py:79
  6.2 2.0 %collective-permute-start.6 = (bf16[640,256]{1,0:T(8,128)(2,1)S(1)}, bf16[640,256]{1,0:T(8,128)(2,1)S(1)}, u32[]{:S(2)}, u32[]{:S(2)}) collective-permute-start(bf16[640,256]{1,0:T(8,128)(2,1)S(1)} %shard_map.121.refs_4_), channel_id=1, source_target_pairs={{0,4},{4,8},{8,12},{12,16},{16,20},{20,24},{24,28},{28,0},{1,5},{5... | collective-permute-start | bytes 983048 | tf_op jit(solution)/shard_map/ppermute | solution.py:47
  8.5 2.8 %collective-permute-start.2 = (bf16[640,256]{1,0:T(8,128)(2,1)S(1)}, bf16[640,256]{1,0:T(8,128)(2,1)S(1)}, u32[]{:S(2)}, u32[]{:S(2)}) collective-permute-start(bf16[640,256]{1,0:T(8,128)(2,1)S(1)} %collective-permute-done.1.refs_3_), channel_id=1, source_target_pairs={{0,4},{4,8},{8,12},{12,16},{16,20},{20,24},{24,28},{28,0},{1,5},{5... | collective-permute-start | bytes 983048 | tf_op jit(solution)/shard_map/ppermute | solution.py:47
  11.4 1.6 %shard_map.122 = (f32[4,256,256]{2,1,0:T(8,128)S(1)}, bf16[4,256,256]{2,1,0:T(8,128)(2,1)S(1)}, bf16[4,256,256]{2,1,0:T(8,128)(2,1)S(1)}, bf16[4,256,256]{2,1,0:T(8,128)(2,1)S(1)}, f32[8,128]{1,0:T(8,128)S(1)}) custom-call(s32[3]{0:T(128)S(1)} %pad_add_fusion.place.refs_0_, bf16[640,1024]{1,0:T(8,128)(2,1)S(1)} %copy-done, ...), custom_call_target="tpu_custom_call" | custom-call | flops 671088640 | bytes 6291456 | tf_op jit(solution)/shard_map/pallas_call | solution.py:79
  13.4 2.6 %collective-permute-start.7 = (bf16[640,256]{1,0:T(8,128)(2,1)S(1)}, bf16[640,256]{1,0:T(8,128)(2,1)S(1)}, u32[]{:S(2)}, u32[]{:S(2)}) collective-permute-start(bf16[640,256]{1,0:T(8,128)(2,1)S(1)} %shard_map.123.refs_4_), channel_id=1, source_target_pairs={{0,4},{4,8},{8,12},{12,16},{16,20},{20,24},{24,28},{28,0},{1,5},{5... | collective-permute-start | bytes 983048 | tf_op jit(solution)/shard_map/ppermute | solution.py:47
  15.9 3.2 %collective-permute-start.10 = (bf16[4,2,128,256]{3,2,1,0:T(8,128)(2,1)S(1)}, bf16[4,2,128,256]{3,2,1,0:T(8,128)(2,1)S(1)}, u32[]{:S(2)}, u32[]{:S(2)}) collective-permute-start(bf16[4,2,128,256]{3,2,1,0:T(8,128)(2,1)S(1)} %get-tuple-element.57), channel_id=1, source_target_pairs={{0,128},{4,132},{8,136},{12,140},{16,144},{20,148},{24,152},{28,15... | collective-permute-start | bytes 1572872 | tf_op jit(solution)/shard_map/ppermute | solution.py:62
  21.2 2.5 %collective-permute-start.3 = (bf16[640,256]{1,0:T(8,128)(2,1)S(1)}, bf16[640,256]{1,0:T(8,128)(2,1)S(1)}, u32[]{:S(2)}, u32[]{:S(2)}) collective-permute-start(bf16[640,256]{1,0:T(8,128)(2,1)S(1)} %collective-permute-done.2.refs_3_), channel_id=1, source_target_pairs={{0,4},{4,8},{8,12},{12,16},{16,20},{20,24},{24,28},{28,0},{1,5},{5... | collective-permute-start | bytes 983048 | tf_op jit(solution)/shard_map/ppermute | solution.py:47
  23.6 1.6 %shard_map.124 = (f32[4,256,256]{2,1,0:T(8,128)S(1)}, bf16[4,256,256]{2,1,0:T(8,128)(2,1)S(1)}, bf16[4,256,256]{2,1,0:T(8,128)(2,1)S(1)}, bf16[4,256,256]{2,1,0:T(8,128)(2,1)S(1)}, f32[8,128]{1,0:T(8,128)S(1)}) custom-call(s32[3]{0:T(128)S(1)} %pad_add_fusion.place.refs_0_, ...), custom_call_target="tpu_custom_call", output_to_operand_aliasing={{0}: (5, {}), {1}: (6, {}), {2}: (7, {}), {3}: (8, {})} | custom-call | flops 671088640 | bytes 6291456 | tf_op jit(solution)/shard_map/pallas_call | solution.py:79
  25.2 2.3 %collective-permute-start.8 = (bf16[640,256]{1,0:T(8,128)(2,1)S(1)}, bf16[640,256]{1,0:T(8,128)(2,1)S(1)}, u32[]{:S(2)}, u32[]{:S(2)}) collective-permute-start(bf16[640,256]{1,0:T(8,128)(2,1)S(1)} %shard_map.125.refs_4_), channel_id=1, source_target_pairs={{0,4},{4,8},{8,12},{12,16},{16,20},{20,24},{24,28},{28,0},{1,5},{5... | collective-permute-start | bytes 983048 | tf_op jit(solution)/shard_map/ppermute | solution.py:47
  28.9 1.8 %shard_map.126 = (f32[4,256,256]{2,1,0:T(8,128)S(1)}, bf16[4,256,256]{2,1,0:T(8,128)(2,1)S(1)}, bf16[4,256,256]{2,1,0:T(8,128)(2,1)S(1)}, bf16[4,256,256]{2,1,0:T(8,128)(2,1)S(1)}, f32[8,128]{1,0:T(8,128)S(1)}) custom-call(s32[3]{0:T(128)S(1)} %pad_add_fusion.place.refs_0_, ...), custom_call_target="tpu_custom_call", output_to_operand_aliasing={{0}: (5, {}), {1}: (6, {}), {2}: (7, {}), {3}: (8, {})} | custom-call | flops 671088640 | bytes 6291456 | tf_op jit(solution)/shard_map/pallas_call | solution.py:79
  30.7 1.9 %collective-permute-done.11.refs_4_.refs_7_ = bf16[4,2,128,256]{3,2,1,0:T(8,128)(2,1)S(1)} collective-permute-done((bf16[4,2,128,256]{3,2,1,0:T(8,128)(2,1)S(1)}, bf16[4,2,128,256]{3,2,1,0:T(8,128)(2,1)S(1)}, u32[]{:S(2)}, u32[]{:S(2)}) %collective-permute-start.11) | collective-permute-done | bytes 524320 | tf_op jit(solution)/shard_map/ppermute | solution.py:62
  33.5 2.2 %shard_map.128 = (f32[4,256,256]{2,1,0:T(8,128)S(1)}, bf16[4,256,256]{2,1,0:T(8,128)(2,1)S(1)}, bf16[4,256,256]{2,1,0:T(8,128)(2,1)S(1)}, bf16[4,256,256]{2,1,0:T(8,128)(2,1)S(1)}, f32[8,128]{1,0:T(8,128)}) custom-call(s32[3]{0:T(128)S(1)} %pad_add_fusion.place.refs_0_, ...), custom_call_target="tpu_custom_call", output_to_operand_aliasing={{0}: (5, {}), {1}: (6, {}), {2}: (7, {}), {3}: (8, {})} | custom-call | flops 671088640 | bytes 6291456 | tf_op jit(solution)/shard_map/pallas_call | solution.py:79
  36.8 1.5 %collective-permute-start.13 = (bf16[4,256,256]{2,1,0:T(8,128)(2,1)S(1)}, bf16[4,256,256]{2,1,0:T(8,128)(2,1)S(1)}, u32[]{:S(2)}, u32[]{:S(2)}) collective-permute-start(bf16[4,256,256]{2,1,0:T(8,128)(2,1)S(1)} %get-tuple-element.68), channel_id=1, source_target_pairs={{0,1},{4,5},{8,9},{12,13},{16,17},{20,21},{24,25},{28,29},{1,2},{5... | collective-permute-start | bytes 1572872 | tf_op jit(solution)/shard_map/ppermute | solution.py:56
  38.3 2.8 %collective-permute-start.14 = (bf16[4,256,256]{2,1,0:T(8,128)(2,1)S(1)}, bf16[4,256,256]{2,1,0:T(8,128)(2,1)S(1)}, u32[]{:S(2)}, u32[]{:S(2)}) collective-permute-start(bf16[4,256,256]{2,1,0:T(8,128)(2,1)S(1)} %get-tuple-element.69), channel_id=1, source_target_pairs={{0,2},{4,6},{8,10},{12,14},{16,18},{20,22},{24,26},{28,30},{1,3},{... | collective-permute-start | bytes 1572872 | tf_op jit(solution)/shard_map/ppermute | solution.py:56
  41.0 1.4 %collective-permute-start.15 = (bf16[4,256,256]{2,1,0:T(8,128)(2,1)S(1)}, bf16[4,256,256]{2,1,0:T(8,128)(2,1)S(1)}, u32[]{:S(2)}, u32[]{:S(2)}) collective-permute-start(bf16[4,256,256]{2,1,0:T(8,128)(2,1)S(1)} %get-tuple-element.70), channel_id=1, source_target_pairs={{0,3},{4,7},{8,11},{12,15},{16,19},{20,23},{24,27},{28,31},{1,0},{... | collective-permute-start | bytes 1572872 | tf_op jit(solution)/shard_map/ppermute | solution.py:56
  44.6 2.5 %collective-permute-done.13.one = bf16[4,256,256]{2,1,0:T(8,128)(2,1)S(1)} collective-permute-done((bf16[4,256,256]{2,1,0:T(8,128)(2,1)S(1)}, bf16[4,256,256]{2,1,0:T(8,128)(2,1)S(1)}, u32[]{:S(2)}, u32[]{:S(2)}) %collective-permute-start.13) | collective-permute-done | bytes 524320 | tf_op jit(solution)/shard_map/ppermute | solution.py:56
  47.2 6.6 %collective-permute-done.14.two = bf16[4,256,256]{2,1,0:T(8,128)(2,1)S(1)} collective-permute-done((bf16[4,256,256]{2,1,0:T(8,128)(2,1)S(1)}, bf16[4,256,256]{2,1,0:T(8,128)(2,1)S(1)}, u32[]{:S(2)}, u32[]{:S(2)}) %collective-permute-start.14) | collective-permute-done | bytes 524320 | tf_op jit(solution)/shard_map/ppermute | solution.py:56
  54.6 1.4 %collective-permute-start.16 = (bf16[256,256]{1,0:T(8,128)(2,1)S(1)}, bf16[256,256]{1,0:T(8,128)(2,1)S(1)}, u32[]{:S(2)}, u32[]{:S(2)}) collective-permute-start(bf16[256,256]{1,0:T(8,128)(2,1)S(1)} %get-tuple-element.72), channel_id=1, source_target_pairs={{0,64},{4,68},{8,72},{12,76},{16,80},{20,84},{24,88},{28,92},{1,65... | collective-permute-start | bytes 393224 | tf_op jit(solution)/shard_map/ppermute | solution.py:62
  56.0 2.8 %collective-permute-start.17 = (bf16[256,256]{1,0:T(8,128)(2,1)S(1)}, bf16[256,256]{1,0:T(8,128)(2,1)S(1)}, u32[]{:S(2)}, u32[]{:S(2)}) collective-permute-start(bf16[256,256]{1,0:T(8,128)(2,1)S(1)} %get-tuple-element.73), channel_id=1, source_target_pairs={{0,128},{4,132},{8,136},{12,140},{16,144},{20,148},{24,152},{28,15... | collective-permute-start | bytes 393224 | tf_op jit(solution)/shard_map/ppermute | solution.py:62
  60.9 2.3 %collective-permute-done.17 = bf16[256,256]{1,0:T(8,128)(2,1)S(1)} collective-permute-done((bf16[256,256]{1,0:T(8,128)(2,1)S(1)}, bf16[256,256]{1,0:T(8,128)(2,1)S(1)}, u32[]{:S(2)}, u32[]{:S(2)}) %collective-permute-start.17) | collective-permute-done | bytes 131104 | tf_op jit(solution)/shard_map/ppermute | solution.py:62
  63.8 5.4 %collective-permute-start.19 = (bf16[256,256]{1,0:T(8,128)(2,1)S(1)}, bf16[256,256]{1,0:T(8,128)(2,1)S(1)}, u32[]{:S(2)}, u32[]{:S(2)}) collective-permute-start(bf16[256,256]{1,0:T(8,128)(2,1)S(1)} %add_convert_fusion), channel_id=1, source_target_pairs={{0,0},{4,36},{8,72},{12,108},{16,144},{20,180},{24,216},{28,252},{... | collective-permute-start | bytes 393224 | tf_op jit(solution)/shard_map/ppermute | solution.py:68
  69.3 5.2 %collective-permute-done.19.gradient = bf16[256,256]{1,0:T(8,128)(2,1)S(1)} collective-permute-done((bf16[256,256]{1,0:T(8,128)(2,1)S(1)}, bf16[256,256]{1,0:T(8,128)(2,1)S(1)}, u32[]{:S(2)}, u32[]{:S(2)}) %collective-permute-start.19) | collective-permute-done | bytes 131104 | tf_op jit(solution)/shard_map/ppermute | solution.py:68
  75.6 1.3 %collective-permute-done.20 = bf16[256,256]{1,0:T(8,128)(2,1)S(1)} collective-permute-done((bf16[256,256]{1,0:T(8,128)(2,1)S(1)}, bf16[256,256]{1,0:T(8,128)(2,1)S(1)}, u32[]{:S(2)}, u32[]{:S(2)}) %collective-permute-start.20) | collective-permute-done | bytes 131104 | tf_op jit(solution)/shard_map/ppermute | solution.py:43
  77.0 2.7 %collective-permute-start.21 = (bf16[2,256,256]{2,1,0:T(8,128)(2,1)S(1)}, bf16[2,256,256]{2,1,0:T(8,128)(2,1)S(1)}, u32[]{:S(2)}, u32[]{:S(2)}) collective-permute-start(bf16[2,256,256]{2,1,0:T(8,128)(2,1)S(1)} %pad_maximum_fusion.refs_0_), channel_id=1, source_target_pairs={{0,3},{4,7},{8,11},{12,15},{16,19},{20,23},{24,27},{28,31},{1,0},{... | collective-permute-start | bytes 786440 | tf_op jit(solution)/shard_map/ppermute | solution.py:56
  80.8 5.6 %collective-permute-done.21.refs_1_ = bf16[2,256,256]{2,1,0:T(8,128)(2,1)S(1)} collective-permute-done((bf16[2,256,256]{2,1,0:T(8,128)(2,1)S(1)}, bf16[2,256,256]{2,1,0:T(8,128)(2,1)S(1)}, u32[]{:S(2)}, u32[]{:S(2)}) %collective-permute-start.21) | collective-permute-done | bytes 262176 | tf_op jit(solution)/shard_map/ppermute | solution.py:56
  87.6 2.7 %collective-permute-done.23.refs_3_ = bf16[2,256,256]{2,1,0:T(8,128)(2,1)S(1)} collective-permute-done((bf16[2,256,256]{2,1,0:T(8,128)(2,1)S(1)}, bf16[2,256,256]{2,1,0:T(8,128)(2,1)S(1)}, u32[]{:S(2)}, u32[]{:S(2)}) %collective-permute-start.23) | collective-permute-done | bytes 262176 | tf_op jit(solution)/shard_map/ppermute | solution.py:56
  91.1 4.8 %collective-permute-start.24 = (bf16[128,256]{1,0:T(8,128)(2,1)S(1)}, bf16[128,256]{1,0:T(8,128)(2,1)S(1)}, u32[]{:S(2)}, u32[]{:S(2)}) collective-permute-start(bf16[128,256]{1,0:T(8,128)(2,1)S(1)} %get-tuple-element.81), channel_id=1, source_target_pairs={{0,192},{4,196},{8,200},{12,204},{16,208},{20,212},{24,216},{28,22... | collective-permute-start | bytes 196616 | tf_op jit(solution)/shard_map/ppermute | solution.py:62
  95.9 3.6 %collective-permute-start.25 = (bf16[128,256]{1,0:T(8,128)(2,1)S(1)}, bf16[128,256]{1,0:T(8,128)(2,1)S(1)}, u32[]{:S(2)}, u32[]{:S(2)}) collective-permute-start(bf16[128,256]{1,0:T(8,128)(2,1)S(1)} %get-tuple-element.82), channel_id=1, source_target_pairs={{0,128},{4,132},{8,136},{12,140},{16,144},{20,148},{24,152},{28,15... | collective-permute-start | bytes 196616 | tf_op jit(solution)/shard_map/ppermute | solution.py:62
  101.8 3.2 %collective-permute-done.26.three = bf16[128,256]{1,0:T(8,128)(2,1)S(1)} collective-permute-done((bf16[128,256]{1,0:T(8,128)(2,1)S(1)}, bf16[128,256]{1,0:T(8,128)(2,1)S(1)}, u32[]{:S(2)}, u32[]{:S(2)}) %collective-permute-start.26) | collective-permute-done | bytes 65568 | tf_op jit(solution)/shard_map/ppermute | solution.py:62
  105.0 1.9 %shard_map.133 = bf16[128,1024]{1,0:T(8,128)(2,1)} custom-call(f32[128,256]{1,0:T(8,128)S(1)} %get-tuple-element.80.own, bf16[128,256]{1,0:T(8,128)(2,1)S(1)} %collective-permute-done.24.one, bf16[128,256]{1,0:T(8,128)(2,1)S(1)} %collective-permute-done.25.two, bf16[128,256]{1,0:T(8,128)(2,1)S(1)} %collective-permute-done.26.three, ...), custom_call_target="tpu_custom_call" | custom-call | bytes 1048576 | tf_op jit(solution)/shard_map/pallas_call | solution.py:79
  (65 shorter events, 19.0 us)
Async XLA Ops:
  0.6 10.7 %copy-start = (bf16[640,1024]{1,0:T(8,128)(2,1)S(1)}, bf16[640,1024]{1,0:T(8,128)(2,1)}, u32[]{:S(2)}) copy-start(bf16[640,1024]{1,0:T(8,128)(2,1)} %refs_1_.9) | copy-start | bytes 3932164
  0.6 10.7 %collective-permute-start = (bf16[640,1024]{1,0:T(8,128)(2,1)}, bf16[640,1024]{1,0:T(8,128)(2,1)S(1)}, u32[]{:S(2)}, u32[]{:S(2)}) collective-permute-start(bf16[640,1024]{1,0:T(8,128)(2,1)} %refs_1_.9), channel_id=1, source_target_pairs={{0,32},{4,36},{8,40},{12,44},{16,48},{20,52},{24,56},{28,60},{1,33... | collective-permute-start | bytes 3932168 | tf_op jit(solution)/shard_map/ppermute | solution.py:43
  0.7 5.5 %collective-permute-start.5 = (bf16[640,256]{1,0:T(8,128)(2,1)}, bf16[640,256]{1,0:T(8,128)(2,1)S(1)}, u32[]{:S(2)}, u32[]{:S(2)}) collective-permute-start(bf16[640,256]{1,0:T(8,128)(2,1)} %refs_3_.1), channel_id=1, source_target_pairs={{0,32},{4,36},{8,40},{12,44},{16,48},{20,52},{24,56},{28,60},{1,33... | collective-permute-start | bytes 983048 | tf_op jit(solution)/shard_map/ppermute | solution.py:43
  1.2 7.3 %collective-permute-start.1 = (bf16[640,256]{1,0:T(8,128)(2,1)}, bf16[640,256]{1,0:T(8,128)(2,1)S(1)}, u32[]{:S(2)}, u32[]{:S(2)}) collective-permute-start(bf16[640,256]{1,0:T(8,128)(2,1)} %refs_3_.1), channel_id=1, source_target_pairs={{0,4},{4,8},{8,12},{12,16},{16,20},{20,24},{24,28},{28,0},{1,5},{5... | collective-permute-start | bytes 983048 | tf_op jit(solution)/shard_map/ppermute | solution.py:47
  6.2 7.2 %collective-permute-start.6 = (bf16[640,256]{1,0:T(8,128)(2,1)S(1)}, bf16[640,256]{1,0:T(8,128)(2,1)S(1)}, u32[]{:S(2)}, u32[]{:S(2)}) collective-permute-start(bf16[640,256]{1,0:T(8,128)(2,1)S(1)} %shard_map.121.refs_4_), channel_id=1, source_target_pairs={{0,4},{4,8},{8,12},{12,16},{16,20},{20,24},{24,28},{28,0},{1,5},{5... | collective-permute-start | bytes 983048 | tf_op jit(solution)/shard_map/ppermute | solution.py:47
  8.5 12.6 %collective-permute-start.2 = (bf16[640,256]{1,0:T(8,128)(2,1)S(1)}, bf16[640,256]{1,0:T(8,128)(2,1)S(1)}, u32[]{:S(2)}, u32[]{:S(2)}) collective-permute-start(bf16[640,256]{1,0:T(8,128)(2,1)S(1)} %collective-permute-done.1.refs_3_), channel_id=1, source_target_pairs={{0,4},{4,8},{8,12},{12,16},{16,20},{20,24},{24,28},{28,0},{1,5},{5... | collective-permute-start | bytes 983048 | tf_op jit(solution)/shard_map/ppermute | solution.py:47
  13.4 11.9 %collective-permute-start.7 = (bf16[640,256]{1,0:T(8,128)(2,1)S(1)}, bf16[640,256]{1,0:T(8,128)(2,1)S(1)}, u32[]{:S(2)}, u32[]{:S(2)}) collective-permute-start(bf16[640,256]{1,0:T(8,128)(2,1)S(1)} %shard_map.123.refs_4_), channel_id=1, source_target_pairs={{0,4},{4,8},{8,12},{12,16},{16,20},{20,24},{24,28},{28,0},{1,5},{5... | collective-permute-start | bytes 983048 | tf_op jit(solution)/shard_map/ppermute | solution.py:47
  15.9 14.8 %collective-permute-start.10 = (bf16[4,2,128,256]{3,2,1,0:T(8,128)(2,1)S(1)}, bf16[4,2,128,256]{3,2,1,0:T(8,128)(2,1)S(1)}, u32[]{:S(2)}, u32[]{:S(2)}) collective-permute-start(bf16[4,2,128,256]{3,2,1,0:T(8,128)(2,1)S(1)} %get-tuple-element.57), channel_id=1, source_target_pairs={{0,128},{4,132},{8,136},{12,140},{16,144},{20,148},{24,152},{28,15... | collective-permute-start | bytes 1572872 | tf_op jit(solution)/shard_map/ppermute | solution.py:62
  19.1 13.5 %collective-permute-start.11 = (bf16[4,2,128,256]{3,2,1,0:T(8,128)(2,1)S(1)}, bf16[4,2,128,256]{3,2,1,0:T(8,128)(2,1)S(1)}, u32[]{:S(2)}, u32[]{:S(2)}) collective-permute-start(bf16[4,2,128,256]{3,2,1,0:T(8,128)(2,1)S(1)} %get-tuple-element.58), channel_id=1, source_target_pairs={{0,192},{4,196},{8,200},{12,204},{16,208},{20,212},{24,216},{28,22... | collective-permute-start | bytes 1572872 | tf_op jit(solution)/shard_map/ppermute | solution.py:62
  20.2 12.4 %collective-permute-start.9 = (bf16[4,2,128,256]{3,2,1,0:T(8,128)(2,1)S(1)}, bf16[4,2,128,256]{3,2,1,0:T(8,128)(2,1)S(1)}, u32[]{:S(2)}, u32[]{:S(2)}) collective-permute-start(bf16[4,2,128,256]{3,2,1,0:T(8,128)(2,1)S(1)} %get-tuple-element.56), channel_id=1, source_target_pairs={{0,64},{4,68},{8,72},{12,76},{16,80},{20,84},{24,88},{28,92},{1,65... | collective-permute-start | bytes 1572872 | tf_op jit(solution)/shard_map/ppermute | solution.py:62
  21.2 7.1 %collective-permute-start.3 = (bf16[640,256]{1,0:T(8,128)(2,1)S(1)}, bf16[640,256]{1,0:T(8,128)(2,1)S(1)}, u32[]{:S(2)}, u32[]{:S(2)}) collective-permute-start(bf16[640,256]{1,0:T(8,128)(2,1)S(1)} %collective-permute-done.2.refs_3_), channel_id=1, source_target_pairs={{0,4},{4,8},{8,12},{12,16},{16,20},{20,24},{24,28},{28,0},{1,5},{5... | collective-permute-start | bytes 983048 | tf_op jit(solution)/shard_map/ppermute | solution.py:47
  25.2 7.4 %collective-permute-start.8 = (bf16[640,256]{1,0:T(8,128)(2,1)S(1)}, bf16[640,256]{1,0:T(8,128)(2,1)S(1)}, u32[]{:S(2)}, u32[]{:S(2)}) collective-permute-start(bf16[640,256]{1,0:T(8,128)(2,1)S(1)} %shard_map.125.refs_4_), channel_id=1, source_target_pairs={{0,4},{4,8},{8,12},{12,16},{16,20},{20,24},{24,28},{28,0},{1,5},{5... | collective-permute-start | bytes 983048 | tf_op jit(solution)/shard_map/ppermute | solution.py:47
  28.2 7.4 %collective-permute-start.4 = (bf16[640,256]{1,0:T(8,128)(2,1)S(1)}, bf16[640,256]{1,0:T(8,128)(2,1)S(1)}, u32[]{:S(2)}, u32[]{:S(2)}) collective-permute-start(bf16[640,256]{1,0:T(8,128)(2,1)S(1)} %collective-permute-done.3.refs_3_), channel_id=1, source_target_pairs={{32,60},{36,32},{40,36},{44,40},{48,44},{52,48},{56,52},{60,56},{3... | collective-permute-start | bytes 983048 | tf_op jit(solution)/shard_map/ppermute | solution.py:52
  32.6 3.0 %collective-permute-start.12 = (bf16[640,256]{1,0:T(8,128)(2,1)S(1)}, bf16[640,256]{1,0:T(8,128)(2,1)S(1)}, u32[]{:S(2)}, u32[]{:S(2)}) collective-permute-start(bf16[640,256]{1,0:T(8,128)(2,1)S(1)} %shard_map.127.refs_4_), channel_id=1, source_target_pairs={{32,60},{36,32},{40,36},{44,40},{48,44},{52,48},{56,52},{60,56},{3... | collective-permute-start | bytes 983048 | tf_op jit(solution)/shard_map/ppermute | solution.py:52
  35.6 6.8 %copy-start.7 = (bf16[32,256,256]{2,1,0:T(8,128)(2,1)S(1)}, bf16[32,256,256]{2,1,0:T(8,128)(2,1)}, u32[]{:S(2)}) copy-start(bf16[32,256,256]{2,1,0:T(8,128)(2,1)} %param.16) | copy-start | bytes 12582916
  36.8 10.4 %collective-permute-start.13 = (bf16[4,256,256]{2,1,0:T(8,128)(2,1)S(1)}, bf16[4,256,256]{2,1,0:T(8,128)(2,1)S(1)}, u32[]{:S(2)}, u32[]{:S(2)}) collective-permute-start(bf16[4,256,256]{2,1,0:T(8,128)(2,1)S(1)} %get-tuple-element.68), channel_id=1, source_target_pairs={{0,1},{4,5},{8,9},{12,13},{16,17},{20,21},{24,25},{28,29},{1,2},{5... | collective-permute-start | bytes 1572872 | tf_op jit(solution)/shard_map/ppermute | solution.py:56
  38.3 15.5 %collective-permute-start.14 = (bf16[4,256,256]{2,1,0:T(8,128)(2,1)S(1)}, bf16[4,256,256]{2,1,0:T(8,128)(2,1)S(1)}, u32[]{:S(2)}, u32[]{:S(2)}) collective-permute-start(bf16[4,256,256]{2,1,0:T(8,128)(2,1)S(1)} %get-tuple-element.69), channel_id=1, source_target_pairs={{0,2},{4,6},{8,10},{12,14},{16,18},{20,22},{24,26},{28,30},{1,3},{... | collective-permute-start | bytes 1572872 | tf_op jit(solution)/shard_map/ppermute | solution.py:56
  41.0 12.8 %collective-permute-start.15 = (bf16[4,256,256]{2,1,0:T(8,128)(2,1)S(1)}, bf16[4,256,256]{2,1,0:T(8,128)(2,1)S(1)}, u32[]{:S(2)}, u32[]{:S(2)}) collective-permute-start(bf16[4,256,256]{2,1,0:T(8,128)(2,1)S(1)} %get-tuple-element.70), channel_id=1, source_target_pairs={{0,3},{4,7},{8,11},{12,15},{16,19},{20,23},{24,27},{28,31},{1,0},{... | collective-permute-start | bytes 1572872 | tf_op jit(solution)/shard_map/ppermute | solution.py:56
  44.6 29.9 %copy-start.4 = (f32[256,256]{1,0:T(8,128)S(1)}, f32[256,256]{1,0:T(8,128)}, u32[]{:S(2)}) copy-start(f32[256,256]{1,0:T(8,128)} %master.1) | copy-start | bytes 786436
  44.6 29.9 %copy-start.5 = (bf16[256,256]{1,0:T(8,128)(2,1)S(1)}, bf16[256,256]{1,0:T(8,128)(2,1)}, u32[]{:S(2)}) copy-start(bf16[256,256]{1,0:T(8,128)(2,1)} %first_moment.1) | copy-start | bytes 393220
  44.6 29.9 %copy-start.6 = (bf16[256,256]{1,0:T(8,128)(2,1)S(1)}, bf16[256,256]{1,0:T(8,128)(2,1)}, u32[]{:S(2)}) copy-start(bf16[256,256]{1,0:T(8,128)(2,1)} %second_moment.1) | copy-start | bytes 393220
  54.6 6.3 %collective-permute-start.16 = (bf16[256,256]{1,0:T(8,128)(2,1)S(1)}, bf16[256,256]{1,0:T(8,128)(2,1)S(1)}, u32[]{:S(2)}, u32[]{:S(2)}) collective-permute-start(bf16[256,256]{1,0:T(8,128)(2,1)S(1)} %get-tuple-element.72), channel_id=1, source_target_pairs={{0,64},{4,68},{8,72},{12,76},{16,80},{20,84},{24,88},{28,92},{1,65... | collective-permute-start | bytes 393224 | tf_op jit(solution)/shard_map/ppermute | solution.py:62
  56.0 7.1 %collective-permute-start.17 = (bf16[256,256]{1,0:T(8,128)(2,1)S(1)}, bf16[256,256]{1,0:T(8,128)(2,1)S(1)}, u32[]{:S(2)}, u32[]{:S(2)}) collective-permute-start(bf16[256,256]{1,0:T(8,128)(2,1)S(1)} %get-tuple-element.73), channel_id=1, source_target_pairs={{0,128},{4,132},{8,136},{12,140},{16,144},{20,148},{24,152},{28,15... | collective-permute-start | bytes 393224 | tf_op jit(solution)/shard_map/ppermute | solution.py:62
  58.8 5.0 %collective-permute-start.18 = (bf16[256,256]{1,0:T(8,128)(2,1)S(1)}, bf16[256,256]{1,0:T(8,128)(2,1)S(1)}, u32[]{:S(2)}, u32[]{:S(2)}) collective-permute-start(bf16[256,256]{1,0:T(8,128)(2,1)S(1)} %get-tuple-element.74), channel_id=1, source_target_pairs={{0,192},{4,196},{8,200},{12,204},{16,208},{20,212},{24,216},{28,22... | collective-permute-start | bytes 393224 | tf_op jit(solution)/shard_map/ppermute | solution.py:62
  63.8 10.7 %collective-permute-start.19 = (bf16[256,256]{1,0:T(8,128)(2,1)S(1)}, bf16[256,256]{1,0:T(8,128)(2,1)S(1)}, u32[]{:S(2)}, u32[]{:S(2)}) collective-permute-start(bf16[256,256]{1,0:T(8,128)(2,1)S(1)} %add_convert_fusion), channel_id=1, source_target_pairs={{0,0},{4,36},{8,72},{12,108},{16,144},{20,180},{24,216},{28,252},{... | collective-permute-start | bytes 393224 | tf_op jit(solution)/shard_map/ppermute | solution.py:68
  75.6 1.3 %collective-permute-start.20 = (bf16[256,256]{1,0:T(8,128)(2,1)S(1)}, bf16[256,256]{1,0:T(8,128)(2,1)S(1)}, u32[]{:S(2)}, u32[]{:S(2)}) collective-permute-start(bf16[256,256]{1,0:T(8,128)(2,1)S(1)} %get-tuple-element.78), channel_id=1, source_target_pairs={{0,32},{4,36},{8,40},{12,44},{16,48},{20,52},{24,56},{28,60},{1,33... | collective-permute-start | bytes 393224 | tf_op jit(solution)/shard_map/ppermute | solution.py:43
  77.0 9.4 %collective-permute-start.21 = (bf16[2,256,256]{2,1,0:T(8,128)(2,1)S(1)}, bf16[2,256,256]{2,1,0:T(8,128)(2,1)S(1)}, u32[]{:S(2)}, u32[]{:S(2)}) collective-permute-start(bf16[2,256,256]{2,1,0:T(8,128)(2,1)S(1)} %pad_maximum_fusion.refs_0_), channel_id=1, source_target_pairs={{0,3},{4,7},{8,11},{12,15},{16,19},{20,23},{24,27},{28,31},{1,0},{... | collective-permute-start | bytes 786440 | tf_op jit(solution)/shard_map/ppermute | solution.py:56
  79.7 8.0 %collective-permute-start.22 = (bf16[2,256,256]{2,1,0:T(8,128)(2,1)S(1)}, bf16[2,256,256]{2,1,0:T(8,128)(2,1)S(1)}, u32[]{:S(2)}, u32[]{:S(2)}) collective-permute-start(bf16[2,256,256]{2,1,0:T(8,128)(2,1)S(1)} %pad_maximum_fusion.refs_0_), channel_id=1, source_target_pairs={{0,2},{4,6},{8,10},{12,14},{16,18},{20,22},{24,26},{28,30},{1,3},{... | collective-permute-start | bytes 786440 | tf_op jit(solution)/shard_map/ppermute | solution.py:56
  80.8 9.6 %collective-permute-start.23 = (bf16[2,256,256]{2,1,0:T(8,128)(2,1)S(1)}, bf16[2,256,256]{2,1,0:T(8,128)(2,1)S(1)}, u32[]{:S(2)}, u32[]{:S(2)}) collective-permute-start(bf16[2,256,256]{2,1,0:T(8,128)(2,1)S(1)} %pad_maximum_fusion.refs_0_), channel_id=1, source_target_pairs={{0,1},{4,5},{8,9},{12,13},{16,17},{20,21},{24,25},{28,29},{1,2},{5... | collective-permute-start | bytes 786440 | tf_op jit(solution)/shard_map/ppermute | solution.py:56
  91.1 9.7 %collective-permute-start.24 = (bf16[128,256]{1,0:T(8,128)(2,1)S(1)}, bf16[128,256]{1,0:T(8,128)(2,1)S(1)}, u32[]{:S(2)}, u32[]{:S(2)}) collective-permute-start(bf16[128,256]{1,0:T(8,128)(2,1)S(1)} %get-tuple-element.81), channel_id=1, source_target_pairs={{0,192},{4,196},{8,200},{12,204},{16,208},{20,212},{24,216},{28,22... | collective-permute-start | bytes 196616 | tf_op jit(solution)/shard_map/ppermute | solution.py:62
  95.9 5.8 %collective-permute-start.25 = (bf16[128,256]{1,0:T(8,128)(2,1)S(1)}, bf16[128,256]{1,0:T(8,128)(2,1)S(1)}, u32[]{:S(2)}, u32[]{:S(2)}) collective-permute-start(bf16[128,256]{1,0:T(8,128)(2,1)S(1)} %get-tuple-element.82), channel_id=1, source_target_pairs={{0,128},{4,132},{8,136},{12,140},{16,144},{20,148},{24,152},{28,15... | collective-permute-start | bytes 196616 | tf_op jit(solution)/shard_map/ppermute | solution.py:62
  99.5 5.5 %collective-permute-start.26 = (bf16[128,256]{1,0:T(8,128)(2,1)S(1)}, bf16[128,256]{1,0:T(8,128)(2,1)S(1)}, u32[]{:S(2)}, u32[]{:S(2)}) collective-permute-start(bf16[128,256]{1,0:T(8,128)(2,1)S(1)} %get-tuple-element.83), channel_id=1, source_target_pairs={{0,64},{4,68},{8,72},{12,76},{16,80},{20,84},{24,88},{28,92},{1,65... | collective-permute-start | bytes 196616 | tf_op jit(solution)/shard_map/ppermute | solution.py:62
  (4 other events, 13.4 us)

commit v3 on v2

--- a/solution.py
+++ b/solution.py
@@ -328,7 +328,8 @@
     arrived = (block, other_block)
     for step in range(5):
         if 0 < step < 4:
-            awaited = (tokens[-1], *states[1:]) if step == 3 else (tokens[-1],)
+            awaited = {2: (states[1], states[3]), 3: (states[2],)}.get(step, ())
+            awaited = (tokens[-1], *awaited)
             arrived = (arrived[0], after_all(arrived[1], *awaited))
         if step < 4:
             send = pass_on if step < 3 else pass_last

time: 107 us -> 106 us (level)
    ppermute x1, starting transfers between devices: 5.44 us -> 7.78 us  [to_owner(): lax.ppermute(a, AXES, pairs_of(lambda y, k, x, z: (z // 2, z % 2, x, z +...]
    ppermute x9, waiting for transfers between devices: 9.69 us -> 7.95 us  [shift_second(): lax.ppermute(a, AXES, pairs_of(lambda y, k, x, z: (y + d, k, x, z) if k =...]
    ppermute x9, starting transfers between devices: 20.4 us -> 19 us  [shift_second(): lax.ppermute(a, AXES, pairs_of(lambda y, k, x, z: (y + d, k, x, z) if k =...]
    ppermute x6, starting transfers between devices: 14.1 us -> 12.7 us  [pass_on(): lax.ppermute(a, AXES, pairs_of(lambda y, k, x, z: (y, k, x, z + 1 - 2 * k)))]
  transfers between devices with their start and end apart: 27 -> 27, of which waited for: 16 -> 14; matrix products, arithmetic and copies ran while one was open for 2% -> 2% of each run, Pallas kernels for 8% -> 8%
where the time goes in v3:
time: 106 us
  starting transfers between devices  51.2 us (48%)
  waiting for transfers between devices  35.8 us (34%)
  Pallas kernels  14.1 us (13%)
  local copies, waits for them, and re-layouts  2 us (2%)
  matrix products  1.35 us (1%)
    ppermute x9, starting transfers between devices, shift_second(): lax.ppermute(a, AXES, pairs_of(lambda y, k, x, z: (y + d, k, x, z) if k =...  19 us
    ppermute x6, waiting for transfers between devices, shift_first(): lax.ppermute(a, AXES, pairs_of(lambda y, k, x, z: (y, k, x + d, z) if k =...  18.5 us
    pallas_call x14, Pallas kernels, call(): pl.pallas_call(kernel, out_shape=out, in_specs=in_specs, out_specs=out_sp...  14.1 us
    ppermute x6, starting transfers between devices, pass_on(): lax.ppermute(a, AXES, pairs_of(lambda y, k, x, z: (y, k, x, z + 1 - 2 * k)))  12.7 us
    ppermute x6, starting transfers between devices, shift_first(): lax.ppermute(a, AXES, pairs_of(lambda y, k, x, z: (y, k, x + d, z) if k =...  9.75 us
    ppermute x9, waiting for transfers between devices, shift_second(): lax.ppermute(a, AXES, pairs_of(lambda y, k, x, z: (y + d, k, x, z) if k =...  7.95 us
    ppermute x1, starting transfers between devices, to_owner(): lax.ppermute(a, AXES, pairs_of(lambda y, k, x, z: (z // 2, z % 2, x, z +...  7.78 us
    ppermute x1, waiting for transfers between devices, to_owner(): lax.ppermute(a, AXES, pairs_of(lambda y, k, x, z: (z // 2, z % 2, x, z +...  5.52 us
  transfers between devices with their start and end apart: 27, of which 14 were waited for; matrix products, arithmetic and copies ran while one was open for 2% of the time, Pallas kernels for 8%

profile of v3, /device:TPU:32, one launch (start us, length us, event | category | flops | bytes accessed | tf_op | source)
XLA Modules:
  0.0 106.0 jit_solution(4711426047452156451)
XLA Ops:
  1.2 1.9 %collective-permute-start.1 = (bf16[640,256]{1,0:T(8,128)(2,1)}, bf16[640,256]{1,0:T(8,128)(2,1)S(1)}, u32[]{:S(2)}, u32[]{:S(2)}) collective-permute-start(bf16[640,256]{1,0:T(8,128)(2,1)} %refs_3_.1), channel_id=1, source_target_pairs={{0,4},{4,8},{8,12},{12,16},{16,20},{20,24},{24,28},{28,0},{1,5},{5... | collective-permute-start | bytes 983048 | tf_op jit(solution)/shard_map/ppermute | solution.py:47
  3.2 1.6 %copy-done.1 = bf16[4,32,8192]{2,1,0:T(8,128)(2,1)S(1)} copy-done((bf16[4,32,8192]{2,1,0:T(8,128)(2,1)S(1)}, bf16[4,32,8192]{2,1,0:T(8,128)(2,1)}, u32[]{:S(2)}) %copy-start.1) | copy-done | bytes 2097176
  4.8 1.4 %shard_map.120 = (bf16[4,2,128,256]{3,2,1,0:T(8,128)(2,1)S(1)}, bf16[4,2,128,256]{3,2,1,0:T(8,128)(2,1)S(1)}, bf16[4,2,128,256]{3,2,1,0:T(8,128)(2,1)S(1)}, bf16...) custom-call(s32[3]{0:T(128)S(1)} %pad_add_fusion.place.refs_0_, bf16[128,8192]{1,0:T(8,128)(2,1)S(1)} %bitcast.47), custom_call_target="tpu_custom_call" | custom-call | bytes 4194304 | tf_op jit(solution)/shard_map/pallas_call | solution.py:79
  6.2 2.0 %collective-permute-start.6 = (bf16[640,256]{1,0:T(8,128)(2,1)S(1)}, bf16[640,256]{1,0:T(8,128)(2,1)S(1)}, u32[]{:S(2)}, u32[]{:S(2)}) collective-permute-start(bf16[640,256]{1,0:T(8,128)(2,1)S(1)} %shard_map.121.refs_4_), channel_id=1, source_target_pairs={{0,4},{4,8},{8,12},{12,16},{16,20},{20,24},{24,28},{28,0},{1,5},{5... | collective-permute-start | bytes 983048 | tf_op jit(solution)/shard_map/ppermute | solution.py:47
  8.2 1.6 %collective-permute-start.8 = (bf16[4,2,128,256]{3,2,1,0:T(8,128)(2,1)S(1)}, bf16[4,2,128,256]{3,2,1,0:T(8,128)(2,1)S(1)}, u32[]{:S(2)}, u32[]{:S(2)}) collective-permute-start(bf16[4,2,128,256]{3,2,1,0:T(8,128)(2,1)S(1)} %get-tuple-element.51), channel_id=1, source_target_pairs={{0,64},{4,68},{8,72},{12,76},{16,80},{20,84},{24,88},{28,92},{1,65... | collective-permute-start | bytes 1572872 | tf_op jit(solution)/shard_map/ppermute | solution.py:62
  9.8 1.7 %collective-permute-start.9 = (bf16[4,2,128,256]{3,2,1,0:T(8,128)(2,1)S(1)}, bf16[4,2,128,256]{3,2,1,0:T(8,128)(2,1)S(1)}, u32[]{:S(2)}, u32[]{:S(2)}) collective-permute-start(bf16[4,2,128,256]{3,2,1,0:T(8,128)(2,1)S(1)} %get-tuple-element.52), channel_id=1, source_target_pairs={{0,192},{4,196},{8,200},{12,204},{16,208},{20,212},{24,216},{28,22... | collective-permute-start | bytes 1572872 | tf_op jit(solution)/shard_map/ppermute | solution.py:62
  11.4 3.1 %collective-permute-start.2 = (bf16[640,256]{1,0:T(8,128)(2,1)S(1)}, bf16[640,256]{1,0:T(8,128)(2,1)S(1)}, u32[]{:S(2)}, u32[]{:S(2)}) collective-permute-start(bf16[640,256]{1,0:T(8,128)(2,1)S(1)} %collective-permute-done.1.refs_3_), channel_id=1, source_target_pairs={{0,4},{4,8},{8,12},{12,16},{16,20},{20,24},{24,28},{28,0},{1,5},{5... | collective-permute-start | bytes 983048 | tf_op jit(solution)/shard_map/ppermute | solution.py:47
  14.6 1.6 %shard_map.122 = (f32[4,256,256]{2,1,0:T(8,128)S(1)}, bf16[4,256,256]{2,1,0:T(8,128)(2,1)S(1)}, bf16[4,256,256]{2,1,0:T(8,128)(2,1)S(1)}, bf16[4,256,256]{2,1,0:T(8,128)(2,1)S(1)}, f32[8,128]{1,0:T(8,128)S(1)}) custom-call(s32[3]{0:T(128)S(1)} %pad_add_fusion.place.refs_0_, bf16[640,1024]{1,0:T(8,128)(2,1)S(1)} %copy-done, ...), custom_call_target="tpu_custom_call" | custom-call | flops 671088640 | bytes 6291456 | tf_op jit(solution)/shard_map/pallas_call | solution.py:79
  17.3 2.0 %collective-permute-start.11 = (bf16[4,2,128,256]{3,2,1,0:T(8,128)(2,1)S(1)}, bf16[4,2,128,256]{3,2,1,0:T(8,128)(2,1)S(1)}, u32[]{:S(2)}, u32[]{:S(2)}) collective-permute-start(bf16[4,2,128,256]{3,2,1,0:T(8,128)(2,1)S(1)} %get-tuple-element.58), channel_id=1, source_target_pairs={{0,128},{4,132},{8,136},{12,140},{16,144},{20,148},{24,152},{28,15... | collective-permute-start | bytes 1572872 | tf_op jit(solution)/shard_map/ppermute | solution.py:62
  19.3 2.4 %collective-permute-start.3 = (bf16[640,256]{1,0:T(8,128)(2,1)S(1)}, bf16[640,256]{1,0:T(8,128)(2,1)S(1)}, u32[]{:S(2)}, u32[]{:S(2)}) collective-permute-start(bf16[640,256]{1,0:T(8,128)(2,1)S(1)} %collective-permute-done.2.refs_3_), channel_id=1, source_target_pairs={{0,4},{4,8},{8,12},{12,16},{16,20},{20,24},{24,28},{28,0},{1,5},{5... | collective-permute-start | bytes 983048 | tf_op jit(solution)/shard_map/ppermute | solution.py:47
  21.7 1.6 %shard_map.124 = (f32[4,256,256]{2,1,0:T(8,128)S(1)}, bf16[4,256,256]{2,1,0:T(8,128)(2,1)S(1)}, bf16[4,256,256]{2,1,0:T(8,128)(2,1)S(1)}, bf16[4,256,256]{2,1,0:T(8,128)(2,1)S(1)}, f32[8,128]{1,0:T(8,128)S(1)}) custom-call(s32[3]{0:T(128)S(1)} %pad_add_fusion.place.refs_0_, ...), custom_call_target="tpu_custom_call", output_to_operand_aliasing={{0}: (5, {}), {1}: (6, {}), {2}: (7, {}), {3}: (8, {})} | custom-call | flops 671088640 | bytes 6291456 | tf_op jit(solution)/shard_map/pallas_call | solution.py:79
  23.3 2.2 %collective-permute-start.10 = (bf16[640,256]{1,0:T(8,128)(2,1)S(1)}, bf16[640,256]{1,0:T(8,128)(2,1)S(1)}, u32[]{:S(2)}, u32[]{:S(2)}) collective-permute-start(bf16[640,256]{1,0:T(8,128)(2,1)S(1)} %shard_map.125.refs_4_), channel_id=1, source_target_pairs={{0,4},{4,8},{8,12},{12,16},{16,20},{20,24},{24,28},{28,0},{1,5},{5... | collective-permute-start | bytes 983048 | tf_op jit(solution)/shard_map/ppermute | solution.py:47
  27.5 1.8 %shard_map.126 = (f32[4,256,256]{2,1,0:T(8,128)S(1)}, bf16[4,256,256]{2,1,0:T(8,128)(2,1)S(1)}, bf16[4,256,256]{2,1,0:T(8,128)(2,1)S(1)}, bf16[4,256,256]{2,1,0:T(8,128)(2,1)S(1)}, f32[8,128]{1,0:T(8,128)S(1)}) custom-call(s32[3]{0:T(128)S(1)} %pad_add_fusion.place.refs_0_, ...), custom_call_target="tpu_custom_call", output_to_operand_aliasing={{0}: (5, {}), {1}: (6, {}), {2}: (7, {}), {3}: (8, {})} | custom-call | flops 671088640 | bytes 6291456 | tf_op jit(solution)/shard_map/pallas_call | solution.py:79
  31.3 2.2 %shard_map.128 = (f32[4,256,256]{2,1,0:T(8,128)S(1)}, bf16[4,256,256]{2,1,0:T(8,128)(2,1)S(1)}, bf16[4,256,256]{2,1,0:T(8,128)(2,1)S(1)}, bf16[4,256,256]{2,1,0:T(8,128)(2,1)S(1)}, f32[8,128]{1,0:T(8,128)}) custom-call(s32[3]{0:T(128)S(1)} %pad_add_fusion.place.refs_0_, ...), custom_call_target="tpu_custom_call", output_to_operand_aliasing={{0}: (5, {}), {1}: (6, {}), {2}: (7, {}), {3}: (8, {})} | custom-call | flops 671088640 | bytes 6291456 | tf_op jit(solution)/shard_map/pallas_call | solution.py:79
  34.6 1.4 %collective-permute-start.13 = (bf16[4,256,256]{2,1,0:T(8,128)(2,1)S(1)}, bf16[4,256,256]{2,1,0:T(8,128)(2,1)S(1)}, u32[]{:S(2)}, u32[]{:S(2)}) collective-permute-start(bf16[4,256,256]{2,1,0:T(8,128)(2,1)S(1)} %get-tuple-element.68), channel_id=1, source_target_pairs={{0,1},{4,5},{8,9},{12,13},{16,17},{20,21},{24,25},{28,29},{1,2},{5... | collective-permute-start | bytes 1572872 | tf_op jit(solution)/shard_map/ppermute | solution.py:56
  36.0 2.8 %collective-permute-start.14 = (bf16[4,256,256]{2,1,0:T(8,128)(2,1)S(1)}, bf16[4,256,256]{2,1,0:T(8,128)(2,1)S(1)}, u32[]{:S(2)}, u32[]{:S(2)}) collective-permute-start(bf16[4,256,256]{2,1,0:T(8,128)(2,1)S(1)} %get-tuple-element.69), channel_id=1, source_target_pairs={{0,2},{4,6},{8,10},{12,14},{16,18},{20,22},{24,26},{28,30},{1,3},{... | collective-permute-start | bytes 1572872 | tf_op jit(solution)/shard_map/ppermute | solution.py:56
  38.8 1.4 %collective-permute-start.15 = (bf16[4,256,256]{2,1,0:T(8,128)(2,1)S(1)}, bf16[4,256,256]{2,1,0:T(8,128)(2,1)S(1)}, u32[]{:S(2)}, u32[]{:S(2)}) collective-permute-start(bf16[4,256,256]{2,1,0:T(8,128)(2,1)S(1)} %get-tuple-element.70), channel_id=1, source_target_pairs={{0,3},{4,7},{8,11},{12,15},{16,19},{20,23},{24,27},{28,31},{1,0},{... | collective-permute-start | bytes 1572872 | tf_op jit(solution)/shard_map/ppermute | solution.py:56
  42.4 2.5 %collective-permute-done.13.one = bf16[4,256,256]{2,1,0:T(8,128)(2,1)S(1)} collective-permute-done((bf16[4,256,256]{2,1,0:T(8,128)(2,1)S(1)}, bf16[4,256,256]{2,1,0:T(8,128)(2,1)S(1)}, u32[]{:S(2)}, u32[]{:S(2)}) %collective-permute-start.13) | collective-permute-done | bytes 524320 | tf_op jit(solution)/shard_map/ppermute | solution.py:56
  45.0 6.6 %collective-permute-done.14.two = bf16[4,256,256]{2,1,0:T(8,128)(2,1)S(1)} collective-permute-done((bf16[4,256,256]{2,1,0:T(8,128)(2,1)S(1)}, bf16[4,256,256]{2,1,0:T(8,128)(2,1)S(1)}, u32[]{:S(2)}, u32[]{:S(2)}) %collective-permute-start.14) | collective-permute-done | bytes 524320 | tf_op jit(solution)/shard_map/ppermute | solution.py:56
  53.1 2.7 %collective-permute-start.17 = (bf16[256,256]{1,0:T(8,128)(2,1)S(1)}, bf16[256,256]{1,0:T(8,128)(2,1)S(1)}, u32[]{:S(2)}, u32[]{:S(2)}) collective-permute-start(bf16[256,256]{1,0:T(8,128)(2,1)S(1)} %get-tuple-element.73), channel_id=1, source_target_pairs={{0,128},{4,132},{8,136},{12,140},{16,144},{20,148},{24,152},{28,15... | collective-permute-start | bytes 393224 | tf_op jit(solution)/shard_map/ppermute | solution.py:62
  55.8 1.3 %collective-permute-start.18 = (bf16[256,256]{1,0:T(8,128)(2,1)S(1)}, bf16[256,256]{1,0:T(8,128)(2,1)S(1)}, u32[]{:S(2)}, u32[]{:S(2)}) collective-permute-start(bf16[256,256]{1,0:T(8,128)(2,1)S(1)} %get-tuple-element.74), channel_id=1, source_target_pairs={{0,192},{4,196},{8,200},{12,204},{16,208},{20,212},{24,216},{28,22... | collective-permute-start | bytes 393224 | tf_op jit(solution)/shard_map/ppermute | solution.py:62
  57.2 2.4 %collective-permute-done.16 = bf16[256,256]{1,0:T(8,128)(2,1)S(1)} collective-permute-done((bf16[256,256]{1,0:T(8,128)(2,1)S(1)}, bf16[256,256]{1,0:T(8,128)(2,1)S(1)}, u32[]{:S(2)}, u32[]{:S(2)}) %collective-permute-start.16) | collective-permute-done | bytes 131104 | tf_op jit(solution)/shard_map/ppermute | solution.py:62
  59.6 1.4 %collective-permute-done.17 = bf16[256,256]{1,0:T(8,128)(2,1)S(1)} collective-permute-done((bf16[256,256]{1,0:T(8,128)(2,1)S(1)}, bf16[256,256]{1,0:T(8,128)(2,1)S(1)}, u32[]{:S(2)}, u32[]{:S(2)}) %collective-permute-start.17) | collective-permute-done | bytes 131104 | tf_op jit(solution)/shard_map/ppermute | solution.py:62
  61.0 7.8 %collective-permute-start.19 = (bf16[256,256]{1,0:T(8,128)(2,1)S(1)}, bf16[256,256]{1,0:T(8,128)(2,1)S(1)}, u32[]{:S(2)}, u32[]{:S(2)}) collective-permute-start(bf16[256,256]{1,0:T(8,128)(2,1)S(1)} %add_convert_fusion), channel_id=1, source_target_pairs={{0,0},{4,36},{8,72},{12,108},{16,144},{20,180},{24,216},{28,252},{... | collective-permute-start | bytes 393224 | tf_op jit(solution)/shard_map/ppermute | solution.py:68
  68.8 5.5 %collective-permute-done.19.gradient = bf16[256,256]{1,0:T(8,128)(2,1)S(1)} collective-permute-done((bf16[256,256]{1,0:T(8,128)(2,1)S(1)}, bf16[256,256]{1,0:T(8,128)(2,1)S(1)}, u32[]{:S(2)}, u32[]{:S(2)}) %collective-permute-start.19) | collective-permute-done | bytes 131104 | tf_op jit(solution)/shard_map/ppermute | solution.py:68
  76.8 2.7 %collective-permute-start.21 = (bf16[2,256,256]{2,1,0:T(8,128)(2,1)S(1)}, bf16[2,256,256]{2,1,0:T(8,128)(2,1)S(1)}, u32[]{:S(2)}, u32[]{:S(2)}) collective-permute-start(bf16[2,256,256]{2,1,0:T(8,128)(2,1)S(1)} %pad_maximum_fusion.refs_0_), channel_id=1, source_target_pairs={{0,3},{4,7},{8,11},{12,15},{16,19},{20,23},{24,27},{28,31},{1,0},{... | collective-permute-start | bytes 786440 | tf_op jit(solution)/shard_map/ppermute | solution.py:56
  80.9 5.4 %collective-permute-done.21.refs_1_ = bf16[2,256,256]{2,1,0:T(8,128)(2,1)S(1)} collective-permute-done((bf16[2,256,256]{2,1,0:T(8,128)(2,1)S(1)}, bf16[2,256,256]{2,1,0:T(8,128)(2,1)S(1)}, u32[]{:S(2)}, u32[]{:S(2)}) %collective-permute-start.21) | collective-permute-done | bytes 262176 | tf_op jit(solution)/shard_map/ppermute | solution.py:56
  87.5 2.7 %collective-permute-done.23.refs_3_ = bf16[2,256,256]{2,1,0:T(8,128)(2,1)S(1)} collective-permute-done((bf16[2,256,256]{2,1,0:T(8,128)(2,1)S(1)}, bf16[2,256,256]{2,1,0:T(8,128)(2,1)S(1)}, u32[]{:S(2)}, u32[]{:S(2)}) %collective-permute-start.23) | collective-permute-done | bytes 262176 | tf_op jit(solution)/shard_map/ppermute | solution.py:56
  91.0 2.7 %collective-permute-start.24 = (bf16[128,256]{1,0:T(8,128)(2,1)S(1)}, bf16[128,256]{1,0:T(8,128)(2,1)S(1)}, u32[]{:S(2)}, u32[]{:S(2)}) collective-permute-start(bf16[128,256]{1,0:T(8,128)(2,1)S(1)} %get-tuple-element.81), channel_id=1, source_target_pairs={{0,192},{4,196},{8,200},{12,204},{16,208},{20,212},{24,216},{28,22... | collective-permute-start | bytes 196616 | tf_op jit(solution)/shard_map/ppermute | solution.py:62
  93.7 5.0 %collective-permute-start.25 = (bf16[128,256]{1,0:T(8,128)(2,1)S(1)}, bf16[128,256]{1,0:T(8,128)(2,1)S(1)}, u32[]{:S(2)}, u32[]{:S(2)}) collective-permute-start(bf16[128,256]{1,0:T(8,128)(2,1)S(1)} %get-tuple-element.82), channel_id=1, source_target_pairs={{0,128},{4,132},{8,136},{12,140},{16,144},{20,148},{24,152},{28,15... | collective-permute-start | bytes 196616 | tf_op jit(solution)/shard_map/ppermute | solution.py:62
  100.9 3.2 %collective-permute-done.26.three = bf16[128,256]{1,0:T(8,128)(2,1)S(1)} collective-permute-done((bf16[128,256]{1,0:T(8,128)(2,1)S(1)}, bf16[128,256]{1,0:T(8,128)(2,1)S(1)}, u32[]{:S(2)}, u32[]{:S(2)}) %collective-permute-start.26) | collective-permute-done | bytes 65568 | tf_op jit(solution)/shard_map/ppermute | solution.py:62
  104.2 1.9 %shard_map.133 = bf16[128,1024]{1,0:T(8,128)(2,1)} custom-call(f32[128,256]{1,0:T(8,128)S(1)} %get-tuple-element.80.own, bf16[128,256]{1,0:T(8,128)(2,1)S(1)} %collective-permute-done.24.one, bf16[128,256]{1,0:T(8,128)(2,1)S(1)} %collective-permute-done.25.two, bf16[128,256]{1,0:T(8,128)(2,1)S(1)} %collective-permute-done.26.three, ...), custom_call_target="tpu_custom_call" | custom-call | bytes 1048576 | tf_op jit(solution)/shard_map/pallas_call | solution.py:79
  (65 shorter events, 18.7 us)
Async XLA Ops:
  0.6 14.0 %copy-start = (bf16[640,1024]{1,0:T(8,128)(2,1)S(1)}, bf16[640,1024]{1,0:T(8,128)(2,1)}, u32[]{:S(2)}) copy-start(bf16[640,1024]{1,0:T(8,128)(2,1)} %refs_1_.9) | copy-start | bytes 3932164
  0.6 13.9 %collective-permute-start = (bf16[640,1024]{1,0:T(8,128)(2,1)}, bf16[640,1024]{1,0:T(8,128)(2,1)S(1)}, u32[]{:S(2)}, u32[]{:S(2)}) collective-permute-start(bf16[640,1024]{1,0:T(8,128)(2,1)} %refs_1_.9), channel_id=1, source_target_pairs={{0,32},{4,36},{8,40},{12,44},{16,48},{20,52},{24,56},{28,60},{1,33... | collective-permute-start | bytes 3932168 | tf_op jit(solution)/shard_map/ppermute | solution.py:43
  0.7 5.5 %collective-permute-start.5 = (bf16[640,256]{1,0:T(8,128)(2,1)}, bf16[640,256]{1,0:T(8,128)(2,1)S(1)}, u32[]{:S(2)}, u32[]{:S(2)}) collective-permute-start(bf16[640,256]{1,0:T(8,128)(2,1)} %refs_3_.1), channel_id=1, source_target_pairs={{0,32},{4,36},{8,40},{12,44},{16,48},{20,52},{24,56},{28,60},{1,33... | collective-permute-start | bytes 983048 | tf_op jit(solution)/shard_map/ppermute | solution.py:43
  1.2 10.2 %collective-permute-start.1 = (bf16[640,256]{1,0:T(8,128)(2,1)}, bf16[640,256]{1,0:T(8,128)(2,1)S(1)}, u32[]{:S(2)}, u32[]{:S(2)}) collective-permute-start(bf16[640,256]{1,0:T(8,128)(2,1)} %refs_3_.1), channel_id=1, source_target_pairs={{0,4},{4,8},{8,12},{12,16},{16,20},{20,24},{24,28},{28,0},{1,5},{5... | collective-permute-start | bytes 983048 | tf_op jit(solution)/shard_map/ppermute | solution.py:47
  4.8 9.8 %copy-start.3 = (bf16[640,256]{1,0:T(8,128)(2,1)S(1)}, bf16[640,256]{1,0:T(8,128)(2,1)}, u32[]{:S(2)}) copy-start(bf16[640,256]{1,0:T(8,128)(2,1)} %refs_3_.1) | copy-start | bytes 983044
  6.2 9.9 %collective-permute-start.6 = (bf16[640,256]{1,0:T(8,128)(2,1)S(1)}, bf16[640,256]{1,0:T(8,128)(2,1)S(1)}, u32[]{:S(2)}, u32[]{:S(2)}) collective-permute-start(bf16[640,256]{1,0:T(8,128)(2,1)S(1)} %shard_map.121.refs_4_), channel_id=1, source_target_pairs={{0,4},{4,8},{8,12},{12,16},{16,20},{20,24},{24,28},{28,0},{1,5},{5... | collective-permute-start | bytes 983048 | tf_op jit(solution)/shard_map/ppermute | solution.py:47
  8.2 15.0 %collective-permute-start.8 = (bf16[4,2,128,256]{3,2,1,0:T(8,128)(2,1)S(1)}, bf16[4,2,128,256]{3,2,1,0:T(8,128)(2,1)S(1)}, u32[]{:S(2)}, u32[]{:S(2)}) collective-permute-start(bf16[4,2,128,256]{3,2,1,0:T(8,128)(2,1)S(1)} %get-tuple-element.51), channel_id=1, source_target_pairs={{0,64},{4,68},{8,72},{12,76},{16,80},{20,84},{24,88},{28,92},{1,65... | collective-permute-start | bytes 1572872 | tf_op jit(solution)/shard_map/ppermute | solution.py:62
  9.8 13.5 %collective-permute-start.9 = (bf16[4,2,128,256]{3,2,1,0:T(8,128)(2,1)S(1)}, bf16[4,2,128,256]{3,2,1,0:T(8,128)(2,1)S(1)}, u32[]{:S(2)}, u32[]{:S(2)}) collective-permute-start(bf16[4,2,128,256]{3,2,1,0:T(8,128)(2,1)S(1)} %get-tuple-element.52), channel_id=1, source_target_pairs={{0,192},{4,196},{8,200},{12,204},{16,208},{20,212},{24,216},{28,22... | collective-permute-start | bytes 1572872 | tf_op jit(solution)/shard_map/ppermute | solution.py:62
  11.4 7.8 %collective-permute-start.2 = (bf16[640,256]{1,0:T(8,128)(2,1)S(1)}, bf16[640,256]{1,0:T(8,128)(2,1)S(1)}, u32[]{:S(2)}, u32[]{:S(2)}) collective-permute-start(bf16[640,256]{1,0:T(8,128)(2,1)S(1)} %collective-permute-done.1.refs_3_), channel_id=1, source_target_pairs={{0,4},{4,8},{8,12},{12,16},{16,20},{20,24},{24,28},{28,0},{1,5},{5... | collective-permute-start | bytes 983048 | tf_op jit(solution)/shard_map/ppermute | solution.py:47
  16.2 7.2 %collective-permute-start.7 = (bf16[640,256]{1,0:T(8,128)(2,1)S(1)}, bf16[640,256]{1,0:T(8,128)(2,1)S(1)}, u32[]{:S(2)}, u32[]{:S(2)}) collective-permute-start(bf16[640,256]{1,0:T(8,128)(2,1)S(1)} %shard_map.123.refs_4_), channel_id=1, source_target_pairs={{0,4},{4,8},{8,12},{12,16},{16,20},{20,24},{24,28},{28,0},{1,5},{5... | collective-permute-start | bytes 983048 | tf_op jit(solution)/shard_map/ppermute | solution.py:47
  17.3 12.0 %collective-permute-start.11 = (bf16[4,2,128,256]{3,2,1,0:T(8,128)(2,1)S(1)}, bf16[4,2,128,256]{3,2,1,0:T(8,128)(2,1)S(1)}, u32[]{:S(2)}, u32[]{:S(2)}) collective-permute-start(bf16[4,2,128,256]{3,2,1,0:T(8,128)(2,1)S(1)} %get-tuple-element.58), channel_id=1, source_target_pairs={{0,128},{4,132},{8,136},{12,140},{16,144},{20,148},{24,152},{28,15... | collective-permute-start | bytes 1572872 | tf_op jit(solution)/shard_map/ppermute | solution.py:62
  19.3 7.6 %collective-permute-start.3 = (bf16[640,256]{1,0:T(8,128)(2,1)S(1)}, bf16[640,256]{1,0:T(8,128)(2,1)S(1)}, u32[]{:S(2)}, u32[]{:S(2)}) collective-permute-start(bf16[640,256]{1,0:T(8,128)(2,1)S(1)} %collective-permute-done.2.refs_3_), channel_id=1, source_target_pairs={{0,4},{4,8},{8,12},{12,16},{16,20},{20,24},{24,28},{28,0},{1,5},{5... | collective-permute-start | bytes 983048 | tf_op jit(solution)/shard_map/ppermute | solution.py:47
  23.3 7.1 %collective-permute-start.10 = (bf16[640,256]{1,0:T(8,128)(2,1)S(1)}, bf16[640,256]{1,0:T(8,128)(2,1)S(1)}, u32[]{:S(2)}, u32[]{:S(2)}) collective-permute-start(bf16[640,256]{1,0:T(8,128)(2,1)S(1)} %shard_map.125.refs_4_), channel_id=1, source_target_pairs={{0,4},{4,8},{8,12},{12,16},{16,20},{20,24},{24,28},{28,0},{1,5},{5... | collective-permute-start | bytes 983048 | tf_op jit(solution)/shard_map/ppermute | solution.py:47
  26.8 6.6 %collective-permute-start.4 = (bf16[640,256]{1,0:T(8,128)(2,1)S(1)}, bf16[640,256]{1,0:T(8,128)(2,1)S(1)}, u32[]{:S(2)}, u32[]{:S(2)}) collective-permute-start(bf16[640,256]{1,0:T(8,128)(2,1)S(1)} %collective-permute-done.3.refs_3_), channel_id=1, source_target_pairs={{32,60},{36,32},{40,36},{44,40},{48,44},{52,48},{56,52},{60,56},{3... | collective-permute-start | bytes 983048 | tf_op jit(solution)/shard_map/ppermute | solution.py:52
  30.4 3.0 %collective-permute-start.12 = (bf16[640,256]{1,0:T(8,128)(2,1)S(1)}, bf16[640,256]{1,0:T(8,128)(2,1)S(1)}, u32[]{:S(2)}, u32[]{:S(2)}) collective-permute-start(bf16[640,256]{1,0:T(8,128)(2,1)S(1)} %shard_map.127.refs_4_), channel_id=1, source_target_pairs={{32,60},{36,32},{40,36},{44,40},{48,44},{52,48},{56,52},{60,56},{3... | collective-permute-start | bytes 983048 | tf_op jit(solution)/shard_map/ppermute | solution.py:52
  34.6 10.4 %collective-permute-start.13 = (bf16[4,256,256]{2,1,0:T(8,128)(2,1)S(1)}, bf16[4,256,256]{2,1,0:T(8,128)(2,1)S(1)}, u32[]{:S(2)}, u32[]{:S(2)}) collective-permute-start(bf16[4,256,256]{2,1,0:T(8,128)(2,1)S(1)} %get-tuple-element.68), channel_id=1, source_target_pairs={{0,1},{4,5},{8,9},{12,13},{16,17},{20,21},{24,25},{28,29},{1,2},{5... | collective-permute-start | bytes 1572872 | tf_op jit(solution)/shard_map/ppermute | solution.py:56
  36.0 15.6 %collective-permute-start.14 = (bf16[4,256,256]{2,1,0:T(8,128)(2,1)S(1)}, bf16[4,256,256]{2,1,0:T(8,128)(2,1)S(1)}, u32[]{:S(2)}, u32[]{:S(2)}) collective-permute-start(bf16[4,256,256]{2,1,0:T(8,128)(2,1)S(1)} %get-tuple-element.69), channel_id=1, source_target_pairs={{0,2},{4,6},{8,10},{12,14},{16,18},{20,22},{24,26},{28,30},{1,3},{... | collective-permute-start | bytes 1572872 | tf_op jit(solution)/shard_map/ppermute | solution.py:56
  38.8 12.8 %collective-permute-start.15 = (bf16[4,256,256]{2,1,0:T(8,128)(2,1)S(1)}, bf16[4,256,256]{2,1,0:T(8,128)(2,1)S(1)}, u32[]{:S(2)}, u32[]{:S(2)}) collective-permute-start(bf16[4,256,256]{2,1,0:T(8,128)(2,1)S(1)} %get-tuple-element.70), channel_id=1, source_target_pairs={{0,3},{4,7},{8,11},{12,15},{16,19},{20,23},{24,27},{28,31},{1,0},{... | collective-permute-start | bytes 1572872 | tf_op jit(solution)/shard_map/ppermute | solution.py:56
  42.4 32.0 %copy-start.4 = (f32[256,256]{1,0:T(8,128)S(1)}, f32[256,256]{1,0:T(8,128)}, u32[]{:S(2)}) copy-start(f32[256,256]{1,0:T(8,128)} %master.1) | copy-start | bytes 786436
  42.4 32.0 %copy-start.5 = (bf16[256,256]{1,0:T(8,128)(2,1)S(1)}, bf16[256,256]{1,0:T(8,128)(2,1)}, u32[]{:S(2)}) copy-start(bf16[256,256]{1,0:T(8,128)(2,1)} %first_moment.1) | copy-start | bytes 393220
  42.4 31.9 %copy-start.6 = (bf16[256,256]{1,0:T(8,128)(2,1)S(1)}, bf16[256,256]{1,0:T(8,128)(2,1)}, u32[]{:S(2)}) copy-start(bf16[256,256]{1,0:T(8,128)(2,1)} %second_moment.1) | copy-start | bytes 393220
  52.4 7.2 %collective-permute-start.16 = (bf16[256,256]{1,0:T(8,128)(2,1)S(1)}, bf16[256,256]{1,0:T(8,128)(2,1)S(1)}, u32[]{:S(2)}, u32[]{:S(2)}) collective-permute-start(bf16[256,256]{1,0:T(8,128)(2,1)S(1)} %get-tuple-element.72), channel_id=1, source_target_pairs={{0,64},{4,68},{8,72},{12,76},{16,80},{20,84},{24,88},{28,92},{1,65... | collective-permute-start | bytes 393224 | tf_op jit(solution)/shard_map/ppermute | solution.py:62
  53.1 7.9 %collective-permute-start.17 = (bf16[256,256]{1,0:T(8,128)(2,1)S(1)}, bf16[256,256]{1,0:T(8,128)(2,1)S(1)}, u32[]{:S(2)}, u32[]{:S(2)}) collective-permute-start(bf16[256,256]{1,0:T(8,128)(2,1)S(1)} %get-tuple-element.73), channel_id=1, source_target_pairs={{0,128},{4,132},{8,136},{12,140},{16,144},{20,148},{24,152},{28,15... | collective-permute-start | bytes 393224 | tf_op jit(solution)/shard_map/ppermute | solution.py:62
  55.8 5.1 %collective-permute-start.18 = (bf16[256,256]{1,0:T(8,128)(2,1)S(1)}, bf16[256,256]{1,0:T(8,128)(2,1)S(1)}, u32[]{:S(2)}, u32[]{:S(2)}) collective-permute-start(bf16[256,256]{1,0:T(8,128)(2,1)S(1)} %get-tuple-element.74), channel_id=1, source_target_pairs={{0,192},{4,196},{8,200},{12,204},{16,208},{20,212},{24,216},{28,22... | collective-permute-start | bytes 393224 | tf_op jit(solution)/shard_map/ppermute | solution.py:62
  61.0 13.3 %collective-permute-start.19 = (bf16[256,256]{1,0:T(8,128)(2,1)S(1)}, bf16[256,256]{1,0:T(8,128)(2,1)S(1)}, u32[]{:S(2)}, u32[]{:S(2)}) collective-permute-start(bf16[256,256]{1,0:T(8,128)(2,1)S(1)} %add_convert_fusion), channel_id=1, source_target_pairs={{0,0},{4,36},{8,72},{12,108},{16,144},{20,180},{24,216},{28,252},{... | collective-permute-start | bytes 393224 | tf_op jit(solution)/shard_map/ppermute | solution.py:68
  75.4 1.3 %collective-permute-start.20 = (bf16[256,256]{1,0:T(8,128)(2,1)S(1)}, bf16[256,256]{1,0:T(8,128)(2,1)S(1)}, u32[]{:S(2)}, u32[]{:S(2)}) collective-permute-start(bf16[256,256]{1,0:T(8,128)(2,1)S(1)} %get-tuple-element.78), channel_id=1, source_target_pairs={{0,32},{4,36},{8,40},{12,44},{16,48},{20,52},{24,56},{28,60},{1,33... | collective-permute-start | bytes 393224 | tf_op jit(solution)/shard_map/ppermute | solution.py:43
  76.8 9.5 %collective-permute-start.21 = (bf16[2,256,256]{2,1,0:T(8,128)(2,1)S(1)}, bf16[2,256,256]{2,1,0:T(8,128)(2,1)S(1)}, u32[]{:S(2)}, u32[]{:S(2)}) collective-permute-start(bf16[2,256,256]{2,1,0:T(8,128)(2,1)S(1)} %pad_maximum_fusion.refs_0_), channel_id=1, source_target_pairs={{0,3},{4,7},{8,11},{12,15},{16,19},{20,23},{24,27},{28,31},{1,0},{... | collective-permute-start | bytes 786440 | tf_op jit(solution)/shard_map/ppermute | solution.py:56
  79.5 8.0 %collective-permute-start.22 = (bf16[2,256,256]{2,1,0:T(8,128)(2,1)S(1)}, bf16[2,256,256]{2,1,0:T(8,128)(2,1)S(1)}, u32[]{:S(2)}, u32[]{:S(2)}) collective-permute-start(bf16[2,256,256]{2,1,0:T(8,128)(2,1)S(1)} %pad_maximum_fusion.refs_0_), channel_id=1, source_target_pairs={{0,2},{4,6},{8,10},{12,14},{16,18},{20,22},{24,26},{28,30},{1,3},{... | collective-permute-start | bytes 786440 | tf_op jit(solution)/shard_map/ppermute | solution.py:56
  80.2 10.0 %collective-permute-start.23 = (bf16[2,256,256]{2,1,0:T(8,128)(2,1)S(1)}, bf16[2,256,256]{2,1,0:T(8,128)(2,1)S(1)}, u32[]{:S(2)}, u32[]{:S(2)}) collective-permute-start(bf16[2,256,256]{2,1,0:T(8,128)(2,1)S(1)} %pad_maximum_fusion.refs_0_), channel_id=1, source_target_pairs={{0,1},{4,5},{8,9},{12,13},{16,17},{20,21},{24,25},{28,29},{1,2},{5... | collective-permute-start | bytes 786440 | tf_op jit(solution)/shard_map/ppermute | solution.py:56
  91.0 9.0 %collective-permute-start.24 = (bf16[128,256]{1,0:T(8,128)(2,1)S(1)}, bf16[128,256]{1,0:T(8,128)(2,1)S(1)}, u32[]{:S(2)}, u32[]{:S(2)}) collective-permute-start(bf16[128,256]{1,0:T(8,128)(2,1)S(1)} %get-tuple-element.81), channel_id=1, source_target_pairs={{0,192},{4,196},{8,200},{12,204},{16,208},{20,212},{24,216},{28,22... | collective-permute-start | bytes 196616 | tf_op jit(solution)/shard_map/ppermute | solution.py:62
  93.7 7.2 %collective-permute-start.25 = (bf16[128,256]{1,0:T(8,128)(2,1)S(1)}, bf16[128,256]{1,0:T(8,128)(2,1)S(1)}, u32[]{:S(2)}, u32[]{:S(2)}) collective-permute-start(bf16[128,256]{1,0:T(8,128)(2,1)S(1)} %get-tuple-element.82), channel_id=1, source_target_pairs={{0,128},{4,132},{8,136},{12,140},{16,144},{20,148},{24,152},{28,15... | collective-permute-start | bytes 196616 | tf_op jit(solution)/shard_map/ppermute | solution.py:62
  98.7 5.5 %collective-permute-start.26 = (bf16[128,256]{1,0:T(8,128)(2,1)S(1)}, bf16[128,256]{1,0:T(8,128)(2,1)S(1)}, u32[]{:S(2)}, u32[]{:S(2)}) collective-permute-start(bf16[128,256]{1,0:T(8,128)(2,1)S(1)} %get-tuple-element.83), channel_id=1, source_target_pairs={{0,64},{4,68},{8,72},{12,76},{16,80},{20,84},{24,88},{28,92},{1,65... | collective-permute-start | bytes 196616 | tf_op jit(solution)/shard_map/ppermute | solution.py:62
  (4 other events, 15.6 us)
